TPU v7x, 256 devices: a whole 4x4x8 slice. The times are simulated.
256 devices in a mesh: frame: 8 (over y, x_hi), space: 32 (over x_lo, z, core).
Axes of the slice: x: 4 (x_hi: 2, x_lo: 2; x = x_hi * 2 + x_lo), y: 4, z: 8, core: 2. Of those that a mesh axis runs over, the one named last changes fastest.
Arguments:
- latent: bfloat16 [16, 2048, 1152], P('frame', 'space'), may hold values from -6 to 6
- modulation: float32 [6, 1152], replicated, may hold values from -4 to 4, as said below
- w_spatial: bfloat16 [1152, 3456], P('space'), may hold values from -0.1875 to 0.1875
- w_spatial_out: bfloat16 [1152, 1152], P('space'), may hold values from -0.1875 to 0.1875
- caption_states: bfloat16 [300, 1152], replicated, may hold values from -6 to 6
- w_text_kv: bfloat16 [1152, 2304], P(None, 'space'), may hold values from -0.1875 to 0.1875
- w_cross_q: bfloat16 [1152, 1152], P('space'), may hold values from -0.1875 to 0.1875
- text_len: int32 [1], replicated, may hold values from 61 to 300
- w_time: bfloat16 [1152, 3456], P('space'), may hold values from -0.1875 to 0.1875
- w_time_out: bfloat16 [1152, 1152], P('space'), may hold values from -0.1875 to 0.1875
Outputs:
- result: bfloat16 [16, 2048, 1152], P('frame', 'space')
Inputs may be any that keep to these rules, and one draw needn't show every extreme that they name: `modulation`: rows 0 and 3 are shifts, rows 1 and 4 scales, rows 2 and 5 gates.
All inputs are finite; a program needn't handle non-finite values.
Results may differ from a plain program's by a relative error of at most 0.025.
Values may be sent and summed in bfloat16 or wider, within the bound.
A program may use at most 128 MiB of HBM per device.

v0:
```python
import math

import jax
import jax.numpy as jnp
from jax import lax
from jax.sharding import PartitionSpec as P

D = 1152
HEADS = 16
HD = 72


def modulate(states, shift, gain):
    values = states.astype(jnp.float32)
    row_mean = jnp.mean(values, axis=-1, keepdims=True)
    centred = values - row_mean
    variance = jnp.mean(centred * centred, axis=-1, keepdims=True)
    return (centred * lax.rsqrt(variance + 1e-06) * (1.0 + gain) + shift).astype(jnp.bfloat16)


def attend(query_rows, key_rows, value_rows):
    scores = jnp.dot(query_rows, key_rows.T, preferred_element_type=jnp.float32) / math.sqrt(HD)
    highest = jnp.max(scores, axis=-1, keepdims=True)
    expsum = jnp.exp(scores - highest)
    weights = (expsum / jnp.sum(expsum, axis=-1, keepdims=True)).astype(jnp.bfloat16)
    return jnp.dot(weights, value_rows, preferred_element_type=jnp.float32).astype(jnp.bfloat16)


def spatial_item(query_key_value):
    query_rows, key_rows, value_rows = query_key_value
    row_count = query_rows.shape[0]
    block_rows = min(512, row_count)
    block_list = query_rows.reshape(row_count // block_rows, block_rows, HD)

    def one_block(block):
        return attend(block, key_rows, value_rows)

    return lax.map(one_block, block_list).reshape(row_count, HD)


def project(rows, weight):
    return jnp.dot(
        rows,
        lax.all_gather(weight, "space", axis=0, tiled=True),
        preferred_element_type=jnp.float32,
    )


def local(
    latent,
    modulation,
    w_spatial,
    w_spatial_out,
    caption_states,
    w_text_kv,
    w_cross_q,
    text_len,
    w_time,
    w_time_out,
):
    frame_rows, patch_rows = (latent.shape[0], latent.shape[1])
    tokens = frame_rows * patch_rows
    flat = latent.reshape(tokens, D)
    normed = modulate(flat, modulation[0], modulation[1])
    qkv_s = project(normed, w_spatial).astype(jnp.bfloat16)
    sectioned = qkv_s.reshape(frame_rows, patch_rows, 3, HEADS, HD).transpose(2, 0, 3, 1, 4)
    sectioned = sectioned.reshape(3, frame_rows * HEADS, patch_rows * HD)
    moved = lax.all_to_all(sectioned, "space", split_axis=1, concat_axis=2, tiled=True)
    item_count = moved.shape[1]
    moved = moved.reshape(3, item_count, -1, HD)
    spatial_pass = lax.map(spatial_item, (moved[0], moved[1], moved[2]))
    returned = lax.all_to_all(
        spatial_pass.reshape(item_count, -1), "space", split_axis=1, concat_axis=0, tiled=True
    )
    spatial_rows = (
        returned.reshape(frame_rows, HEADS, patch_rows, HD).transpose(0, 2, 1, 3).reshape(tokens, D)
    )
    spatial_term = project(spatial_rows, w_spatial_out)
    after_space = (flat.astype(jnp.float32) + modulation[2] * spatial_term).astype(jnp.bfloat16)
    local_kv = jnp.dot(caption_states, w_text_kv, preferred_element_type=jnp.float32).astype(
        jnp.bfloat16
    )
    text_kv = lax.all_gather(local_kv, "space", axis=1, tiled=True)
    text_count = text_kv.shape[0]
    text_keys = text_kv[:, :D].reshape(text_count, HEADS, HD)
    text_values = text_kv[:, D:].reshape(text_count, HEADS, HD)
    cross_q = project(after_space, w_cross_q).astype(jnp.bfloat16).reshape(tokens, HEADS, HD)
    valid = jnp.arange(text_count) < text_len[0]
    scores = jnp.einsum(
        "rhe,jhe->hrj", cross_q, text_keys, preferred_element_type=jnp.float32
    ) / math.sqrt(HD)
    scores = jnp.where(valid[None, None, :], scores, -jnp.inf)
    highest = jnp.max(scores, axis=-1, keepdims=True)
    expsum = jnp.exp(scores - highest)
    weights = (expsum / jnp.sum(expsum, axis=-1, keepdims=True)).astype(jnp.bfloat16)
    crossed = jnp.einsum("hrj,jhe->rhe", weights, text_values, preferred_element_type=jnp.float32)
    crossed = crossed.astype(jnp.bfloat16).reshape(tokens, D)
    after_text = (after_space.astype(jnp.float32) + crossed.astype(jnp.float32)).astype(
        jnp.bfloat16
    )
    normed_t = modulate(after_text, modulation[3], modulation[4])
    qkv_t = project(normed_t, w_time).astype(jnp.bfloat16)
    sectioned_t = qkv_t.reshape(frame_rows, patch_rows, 3, HEADS, HD).transpose(2, 1, 3, 0, 4)
    sectioned_t = sectioned_t.reshape(3, patch_rows * HEADS, frame_rows * HD)
    moved_transposed = lax.all_to_all(sectioned_t, "frame", split_axis=1, concat_axis=2, tiled=True)
    time_items = moved_transposed.shape[1]
    moved_transposed = moved_transposed.reshape(3, time_items, -1, HD)
    time_scores = jnp.einsum(
        "iou,icu->ioc", moved_transposed[0], moved_transposed[1], preferred_element_type=jnp.float32
    ) / math.sqrt(HD)
    temporal_upper = jnp.max(time_scores, axis=-1, keepdims=True)
    time_exp = jnp.exp(time_scores - temporal_upper)
    temporal_weights = (time_exp / jnp.sum(time_exp, axis=-1, keepdims=True)).astype(jnp.bfloat16)
    temporal = jnp.einsum(
        "lmo,log->lmg", temporal_weights, moved_transposed[2], preferred_element_type=jnp.float32
    )
    temporal = temporal.astype(jnp.bfloat16).reshape(time_items, -1)
    back_t = lax.all_to_all(temporal, "frame", split_axis=1, concat_axis=0, tiled=True)
    temporal_rows = (
        back_t.reshape(patch_rows, HEADS, frame_rows, HD).transpose(2, 0, 1, 3).reshape(tokens, D)
    )
    time_term = project(temporal_rows, w_time_out)
    result = (after_text.astype(jnp.float32) + modulation[5] * time_term).astype(jnp.bfloat16)
    return result.reshape(frame_rows, patch_rows, D)


def solution(mesh):
    placed = (
        P("frame", "space", None),
        P(),
        P("space", None),
        P("space", None),
        P(),
        P(None, "space"),
        P("space", None),
        P(),
        P("space", None),
        P("space", None),
    )
    return jax.shard_map(
        local, mesh=mesh, in_specs=placed, out_specs=P("frame", "space", None), check_vma=False
    )
```

profile of v0, /device:TPU:1, one launch (start us, length us, event | category | flops | bytes accessed | tf_op | source)
XLA Modules:
  0.0 481.5 jit_solution(16258670415992977970)
XLA Ops:
  16.3 69.7 %all-gather.14.cloned.1.call-done = bf16[32,36,3456]{2,1,0:T(8,128)(2,1)} async-done(((bf16[1,36,3456]{2,1,0:T(8,128)(2,1)}), bf16[32,36,3456]{2,1,0:T(8,128)(2,1)}) %all-gather.14.cloned.1.call-update) | async-done | bytes 7962640 | tf_op jit(solution)/shard_map/all_gather | solution.py:44
  86.0 12.5 %reshape.160 = bf16[1152,3456]{1,0:T(8,128)(2,1)} reshape(bf16[32,36,3456]{2,1,0:T(8,128)(2,1)} %all-gather.14.cloned.1.call-done) | data formatting | bytes 15925248
  98.5 4.6 convolution_convert_fusion.1
  107.5 3.3 reshape.145
  112.6 6.3 %all-to-all-start = ((bf16[3,32,4608]{2,0,1:T(4,128)(2,1)}), bf16[3,32,4608]{2,0,1:T(4,128)(2,1)S(1)}, u32[]{:S(2)}, u32[]{:S(2)}) async-start(bf16[3,32,4608]{2,0,1:T(4,128)(2,1)} %copy.52), calls=%async_computation | async-start | bytes 2359296 | tf_op jit(solution)/shard_map/all_to_all | solution.py:68
  120.1 32.4 %all-to-all-done = bf16[3,32,4608]{2,0,1:T(4,128)(2,1)S(1)} async-done(((bf16[3,32,4608]{2,0,1:T(4,128)(2,1)}), bf16[3,32,4608]{2,0,1:T(4,128)(2,1)S(1)}, u32[]{:S(2)}, u32[]{:S(2)}) %all-to-all-start) | async-done | bytes 884768 | tf_op jit(solution)/shard_map/all_to_all | solution.py:68
  152.5 3.7 slice_reduce_fusion
  159.7 11.0 %while.17 = (s32[]{:T(128)}, bf16[4,512,72]{1,2,0:T(8,128)(2,1)S(1)}, bf16[4,512,72]{2,1,0:T(8,128)(2,1)S(1)}, bf16[2048,72]{1,0:T(8,128)(2,1)S(1)}, bf16[2048,72]{1,0:T(8,128)(2,1)S(1)}, /*index=5*/s32[]{:T(128)}) while((s32[]{:T(128)}, bf16[4,512,72]{1,2,0:T(8,128)(2,1)S(1)}, bf16[4,512,72]{2,1,0:T(8,128)(2,1)S(1)}, ...), condition=%wide.region_5.0_spmd, body=%wide.region_2.5_spmd.sunk | while | flops 311462912 | bytes 13846605 | solution.py:38
  175.7 5.7 %all-to-all-start.1 = ((bf16[32,2,2304]{2,1,0:T(2,128)(2,1)}), bf16[32,2,2304]{2,1,0:T(2,128)(2,1)S(1)}, u32[]{:S(2)}, u32[]{:S(2)}) async-start(bf16[32,2,2304]{2,1,0:T(2,128)(2,1)} %reshape.179), calls=%async_computation.1 | async-start | bytes 589824 | tf_op jit(solution)/shard_map/all_to_all | solution.py:72
  184.3 42.3 %all-gather.16.cloned.1.call-done = bf16[32,36,1152]{2,1,0:T(8,128)(2,1)} async-done(((bf16[1,36,1152]{2,1,0:T(8,128)(2,1)}), bf16[32,36,1152]{2,1,0:T(8,128)(2,1)}) %all-gather.16.cloned.1.call-update) | async-done | bytes 2654224 | tf_op jit(solution)/shard_map/all_gather | solution.py:44
  226.6 3.6 reshape.162
  230.2 63.1 %all-gather.18.cloned.1.call-done = bf16[32,36,1152]{2,1,0:T(8,128)(2,1)} async-done(((bf16[1,36,1152]{2,1,0:T(8,128)(2,1)}), bf16[32,36,1152]{2,1,0:T(8,128)(2,1)}) %all-gather.18.cloned.1.call-update) | async-done | bytes 2654224 | tf_op jit(solution)/shard_map/all_gather | solution.py:44
  293.4 5.2 %reshape.164 = bf16[1152,1152]{1,0:T(8,128)(2,1)} reshape(bf16[32,36,1152]{2,1,0:T(8,128)(2,1)} %all-gather.18.cloned.1.call-done) | data formatting | bytes 5308416
  298.5 68.9 %all-gather.20.cloned.1.call-done = bf16[32,36,3456]{2,1,0:T(8,128)(2,1)} async-done(((bf16[1,36,3456]{2,1,0:T(8,128)(2,1)}), bf16[32,36,3456]{2,1,0:T(8,128)(2,1)}) %all-gather.20.cloned.1.call-update) | async-done | bytes 7962640 | tf_op jit(solution)/shard_map/all_gather | solution.py:44
  367.4 12.4 %reshape.166 = bf16[1152,3456]{1,0:T(8,128)(2,1)} reshape(bf16[32,36,3456]{2,1,0:T(8,128)(2,1)} %all-gather.20.cloned.1.call-done) | data formatting | bytes 15925248
  398.4 4.7 convolution_convert_fusion
  406.2 3.6 copy.76
  409.8 3.8 reshape.153
  416.3 3.4 reshape.181
  419.7 21.8 %all_to_all.54 = bf16[8,2,27648]{2,1,0:T(2,128)(2,1)} all-to-all(bf16[8,2,27648]{2,1,0:T(2,128)(2,1)} %reshape.181), channel_id=1, replica_groups=mesh['frame'=8,'space'=32] {'frame'}, dimensions={0} | all-to-all | bytes 1769472 | tf_op jit(solution)/shard_map/all_to_all | solution.py:105
  441.5 4.0 reshape.182
  453.4 3.4 all-to-all-start.3
  456.9 3.6 reshape.168
  460.5 4.1 all-to-all-done.3
  (100 shorter events, 80.4 us)
Async XLA Ops:
  6.5 1.1 copy-start
  6.5 79.5 %all-gather.14.cloned.1.call-start = ((), (), s32[]{:S(2)}) async-start(), calls=%async_computation.5 | async-start | bytes 9123840 | tf_op jit(solution)/shard_map/all_gather | solution.py:44
  7.3 174.2 %all-gather.12.cloned.1.call-start = ((), (), s32[]{:S(2)}) async-start(), calls=%async_computation.4 | async-start | bytes 1824768 | tf_op jit(solution)/shard_map/all_gather | solution.py:83
  9.6 217.1 %all-gather.16.cloned.1.call-start = ((), (), s32[]{:S(2)}) async-start(), calls=%async_computation.6 | async-start | bytes 3041280 | tf_op jit(solution)/shard_map/all_gather | solution.py:44
  10.3 283.1 %all-gather.18.cloned.1.call-start = ((), (), s32[]{:S(2)}) async-start(), calls=%async_computation.7 | async-start | bytes 3041280 | tf_op jit(solution)/shard_map/all_gather | solution.py:44
  10.9 356.5 %all-gather.20.cloned.1.call-start = ((), (), s32[]{:S(2)}) async-start(), calls=%async_computation.8 | async-start | bytes 9123840 | tf_op jit(solution)/shard_map/all_gather | solution.py:44
  112.6 39.9 %all-to-all-start = ((bf16[3,32,4608]{2,0,1:T(4,128)(2,1)}), bf16[3,32,4608]{2,0,1:T(4,128)(2,1)S(1)}, u32[]{:S(2)}, u32[]{:S(2)}) async-start(bf16[3,32,4608]{2,0,1:T(4,128)(2,1)} %copy.52), calls=%async_computation | async-start | bytes 2359296 | tf_op jit(solution)/shard_map/all_to_all | solution.py:68
  118.9 338.0 %all-gather.22.cloned.1.call-start = ((), (), s32[]{:S(2)}) async-start(), calls=%async_computation.9 | async-start | bytes 3041280 | tf_op jit(solution)/shard_map/all_gather | solution.py:44
  175.7 204.1 %all-to-all-start.1 = ((bf16[32,2,2304]{2,1,0:T(2,128)(2,1)}), bf16[32,2,2304]{2,1,0:T(2,128)(2,1)S(1)}, u32[]{:S(2)}, u32[]{:S(2)}) async-start(bf16[32,2,2304]{2,1,0:T(2,128)(2,1)} %reshape.179), calls=%async_computation.1 | async-start | bytes 589824 | tf_op jit(solution)/shard_map/all_to_all | solution.py:72
  379.8 10.2 %copy-start.4 = (bf16[2,64,1152]{2,1,0:T(8,128)(2,1)S(1)}, bf16[2,64,1152]{2,1,0:T(8,128)(2,1)}, u32[]{:S(2)}) copy-start(bf16[2,64,1152]{2,1,0:T(8,128)(2,1)} %param.12) | copy-start | bytes 884740
  390.0 1.8 copy-start.2
  391.8 1.2 copy-start.7
  392.4 3.1 copy-start.6
  398.1 5.0 %copy-start.3 = (bf16[128,1152]{1,0:T(8,128)(2,1)}, bf16[128,1152]{1,0:T(8,128)(2,1)S(1)}, u32[]{:S(2)}) copy-start(bf16[128,1152]{1,0:T(8,128)(2,1)S(1)} %get-tuple-element.68) | copy-start | bytes 884740
  453.4 11.2 %all-to-all-start.3 = ((bf16[128,8,144]{0,2,1:T(8,128)(2,1)}), bf16[128,8,144]{0,2,1:T(8,128)(2,1)S(1)}, u32[]{:S(2)}, u32[]{:S(2)}) async-start(bf16[128,8,144]{0,2,1:T(8,128)(2,1)} %bitcast.21), calls=%async_computation.3 | async-start | bytes 589824 | tf_op jit(solution)/shard_map/all_to_all | solution.py:118
  464.6 0.7 copy-start.5
  467.6 6.6 %copy-start.1 = (bf16[300,1152]{1,0:T(8,128)(2,1)S(1)}, bf16[300,1152]{1,0:T(8,128)(2,1)}, u32[]{:S(2)}) copy-start(bf16[300,1152]{1,0:T(8,128)(2,1)} %param.16) | copy-start | bytes 2073604
Sparse Core Ops, SparseCore 0:
  9.2 76.7 all-gather.13
  87.8 70.2 all-gather.11
  160.0 66.6 all-gather.15
  228.3 64.9 all-gather.17
  295.1 72.3 all-gather.19
  369.1 65.3 all-gather.21
where the time goes:
time: 489 us; the launch traced here: 481 us
  waiting for transfers between devices  283 us (58%)
  local copies, waits for them, and re-layouts  105 us (21%)
  matrix products  29.9 us (6%)
  blocking collectives  21.8 us (4%)
  starting transfers between devices  15.8 us (3%)
  between operations  14.9 us (3%)
  other arithmetic  10.7 us (2%)
    all_gather x5, waiting for transfers between devices, project(): lax.all_gather(weight, 'space', axis=0, tiled=True)  244 us
    unnamed x26, local copies, waits for them, and re-layouts  48.4 us
    all_to_all x1, waiting for transfers between devices, local(): lax.all_to_all(sectioned, 'space', split_axis=1, concat_axis=2, tiled=True)  32.4 us
    all_to_all x1, blocking collectives, local(): lax.all_to_all(sectioned_t, 'frame', split_axis=1, concat_axis=2, tiled=T...  21.8 us
    dot_general x5, matrix products, project(): jnp.dot(rows, lax.all_gather(weight, 'space', axis=0, tiled=True), prefer...  14.1 us
  transfers between devices with their start and end apart: 9, of which 6 were waited for; matrix products, arithmetic and copies ran while one was open for 28% of the time, Pallas kernels for 0%

commit v1 on v0

--- a/solution.py
+++ b/solution.py
@@ -39,11 +39,7 @@
 
 
 def project(rows, weight):
-    return jnp.dot(
-        rows,
-        lax.all_gather(weight, "space", axis=0, tiled=True),
-        preferred_element_type=jnp.float32,
-    )
+    return jnp.dot(rows, weight, preferred_element_type=jnp.float32)
 
 
 def local(
@@ -61,6 +57,22 @@
     frame_rows, patch_rows = (latent.shape[0], latent.shape[1])
     tokens = frame_rows * patch_rows
     flat = latent.reshape(tokens, D)
+    local_kv = jnp.dot(caption_states, w_text_kv, preferred_element_type=jnp.float32).astype(
+        jnp.bfloat16
+    )
+    shard_rows = w_spatial.shape[0]
+    text_flat = local_kv.reshape(shard_rows, -1)
+    joined = jnp.concatenate(
+        [w_spatial, w_spatial_out, w_cross_q, w_time, w_time_out, text_flat], axis=1
+    )
+    joined = lax.all_gather(joined, "space", axis=0, tiled=True)
+    w_spatial = joined[:, : 3 * D]
+    w_spatial_out = joined[:, 3 * D : 4 * D]
+    w_cross_q = joined[:, 4 * D : 5 * D]
+    w_time = joined[:, 5 * D : 8 * D]
+    w_time_out = joined[:, 8 * D : 9 * D]
+    text_kv = joined[:, 9 * D :].reshape(-1, caption_states.shape[0], local_kv.shape[1])
+    text_kv = text_kv.transpose(1, 0, 2).reshape(caption_states.shape[0], 2 * D)
     normed = modulate(flat, modulation[0], modulation[1])
     qkv_s = project(normed, w_spatial).astype(jnp.bfloat16)
     sectioned = qkv_s.reshape(frame_rows, patch_rows, 3, HEADS, HD).transpose(2, 0, 3, 1, 4)
@@ -77,10 +89,6 @@
     )
     spatial_term = project(spatial_rows, w_spatial_out)
     after_space = (flat.astype(jnp.float32) + modulation[2] * spatial_term).astype(jnp.bfloat16)
-    local_kv = jnp.dot(caption_states, w_text_kv, preferred_element_type=jnp.float32).astype(
-        jnp.bfloat16
-    )
-    text_kv = lax.all_gather(local_kv, "space", axis=1, tiled=True)
     text_count = text_kv.shape[0]
     text_keys = text_kv[:, :D].reshape(text_count, HEADS, HD)
     text_values = text_kv[:, D:].reshape(text_count, HEADS, HD)

time: 489 us -> 397 us (0.81)
  waiting for transfers between devices: 283 us -> 191 us
  blocking collectives: 21.8 us -> 30.5 us
  local copies, waits for them, and re-layouts: 105 us -> 97.4 us
  matrix products: 29.9 us -> 35.1 us
    all_gather x6 -> x1, waiting for transfers between devices: 244 us -> 161 us  [local(): joined = lax.all_gather(joined, 'space', axis=0, tiled=True)]
    all_to_all x0 -> x1, blocking collectives: none -> 10.8 us  [local(): lax.all_to_all(temporal, 'frame', split_axis=1, concat_axis=0, tiled=True)]
    unnamed x26 -> x27, local copies, waits for them, and re-layouts: 48.4 us -> 41.3 us
    reshape x0 -> x2, local copies, waits for them, and re-layouts: none -> 5.58 us  [the longest x1 5.42 us: local(): joined[:, 9 * D:].reshape(-1, caption_states.shape[0], local_kv.shape[1])]
    dot_general x5, matrix products: 14.1 us -> 19.1 us  [project(): return jnp.dot(rows, weight, preferred_element_type=jnp.float32)]
  transfers between devices with their start and end apart: 9 -> 3, of which waited for: 6 -> 3; matrix products, arithmetic and copies ran while one was open for 28% -> 3% of each run, Pallas kernels for 0% -> 0%
where the time goes in v1:
time: 397 us; the launch traced here: 390 us
  waiting for transfers between devices  191 us (48%)
  local copies, waits for them, and re-layouts  97.4 us (25%)
  matrix products  35.1 us (9%)
  blocking collectives  30.5 us (8%)
  between operations  14.7 us (4%)
  starting transfers between devices  14.4 us (4%)
  other arithmetic  6.79 us (2%)
    all_gather x1, waiting for transfers between devices, local(): joined = lax.all_gather(joined, 'space', axis=0, tiled=True)  161 us
    unnamed x27, local copies, waits for them, and re-layouts  41.3 us
    all_to_all x1, waiting for transfers between devices, local(): lax.all_to_all(sectioned, 'space', split_axis=1, concat_axis=2, tiled=True)  28.3 us
    all_to_all x1, blocking collectives, local(): lax.all_to_all(sectioned_t, 'frame', split_axis=1, concat_axis=2, tiled=T...  19.7 us
    dot_general x5, matrix products, project(): return jnp.dot(rows, weight, preferred_element_type=jnp.float32)  19.1 us
    all_to_all x1, blocking collectives, local(): lax.all_to_all(temporal, 'frame', split_axis=1, concat_axis=0, tiled=True)  10.8 us
  transfers between devices with their start and end apart: 3, of which 3 were waited for; matrix products, arithmetic and copies ran while one was open for 3% of the time, Pallas kernels for 0%

profile of v1, /device:TPU:1, one launch (start us, length us, event | category | flops | bytes accessed | tf_op | source)
XLA Modules:
  0.0 389.6 jit_solution(15797043774068869738)
XLA Ops:
  14.0 160.6 %all-gather.3.cloned.1.call-done = bf16[32,36,10968]{2,1,0:T(8,128)(2,1)} async-done(((bf16[1,36,10968]{2,1,0:T(8,128)(2,1)}), bf16[32,36,10968]{2,1,0:T(8,128)(2,1)}) %all-gather.3.cloned.1.call-update) | async-done | bytes 25270288 | tf_op jit(solution)/shard_map/all_gather | solution.py:68
  174.6 27.4 %reshape.172 = bf16[1152,10968]{1,0:T(8,128)(2,1)} reshape(bf16[32,36,10968]{2,1,0:T(8,128)(2,1)} %all-gather.3.cloned.1.call-done) | data formatting | bytes 50540544
  202.0 5.6 %fusion.16 = bf16[128,3456]{1,0:T(8,128)(2,1)} fusion(bf16[128,1152]{1,0:T(8,128)(2,1)S(1)} %fusion.67, bf16[1152,10968]{1,0:T(8,128)(2,1)} %reshape.172), kind=kOutput, calls=%fused_computation.19 | convolution fusion | flops 1019658240 | bytes 9142272 | tf_op jit(solution)/shard_map/dot_general | solution.py:42
  207.6 4.0 %reshape.154 = bf16[2,64,3,16,72]{4,3,2,1,0:T(8,128)(2,1)S(1)} reshape(bf16[128,3456]{1,0:T(8,128)(2,1)} %fusion.16) | data formatting | bytes 1769472 | tf_op jit(solution)/shard_map/reshape | solution.py:78
  213.1 3.3 reshape.155
  218.2 7.9 %all-to-all-start = ((bf16[3,32,4608]{2,0,1:T(4,128)(2,1)}), bf16[3,32,4608]{2,0,1:T(4,128)(2,1)S(1)}, u32[]{:S(2)}, u32[]{:S(2)}) async-start(bf16[3,32,4608]{2,0,1:T(4,128)(2,1)} %copy.76), calls=%async_computation | async-start | bytes 2359296 | tf_op jit(solution)/shard_map/all_to_all | solution.py:80
  226.8 28.3 %all-to-all-done = bf16[3,32,4608]{2,0,1:T(4,128)(2,1)S(1)} async-done(((bf16[3,32,4608]{2,0,1:T(4,128)(2,1)}), bf16[3,32,4608]{2,0,1:T(4,128)(2,1)S(1)}, u32[]{:S(2)}, u32[]{:S(2)}) %all-to-all-start) | async-done | bytes 884768 | tf_op jit(solution)/shard_map/all_to_all | solution.py:80
  255.1 3.7 slice_reduce_fusion
  262.3 11.0 %while.17 = (s32[]{:T(128)}, bf16[4,512,72]{1,2,0:T(8,128)(2,1)S(1)}, bf16[4,512,72]{2,1,0:T(8,128)(2,1)S(1)}, bf16[2048,72]{1,0:T(8,128)(2,1)S(1)}, bf16[2048,72]{1,0:T(8,128)(2,1)S(1)}, /*index=5*/s32[]{:T(128)}) while((s32[]{:T(128)}, bf16[4,512,72]{1,2,0:T(8,128)(2,1)S(1)}, bf16[4,512,72]{2,1,0:T(8,128)(2,1)S(1)}, ...), condition=%wide.region_5.0_spmd, body=%wide.region_2.5_spmd.sunk | while | flops 311462912 | bytes 13846613 | solution.py:38
  278.3 6.4 %all-to-all-start.1 = ((bf16[32,2,2304]{2,1,0:T(2,128)(2,1)}), bf16[32,2,2304]{2,1,0:T(2,128)(2,1)S(1)}, u32[]{:S(2)}, u32[]{:S(2)}) async-start(bf16[32,2,2304]{2,1,0:T(2,128)(2,1)} %reshape.183), calls=%async_computation.1 | async-start | bytes 589824 | tf_op jit(solution)/shard_map/all_to_all | solution.py:84
  284.8 5.4 %reshape.159 = bf16[32,300,72]{2,1,0:T(8,128)(2,1)} reshape(bf16[1152,600]{1,0:T(8,128)(2,1)S(1)} %slice-done) | data formatting | bytes 2764800 | tf_op jit(solution)/shard_map/reshape | solution.py:74
  290.2 3.8 copy.80
  306.2 2.5 fusion.82
  311.5 5.6 %fusion.19 = bf16[128,3456]{1,0:T(8,128)(2,1)} fusion(bf16[1152,10968]{1,0:T(8,128)(2,1)} %reshape.172, bf16[128,1152]{1,0:T(8,128)(2,1)S(1)} %get-tuple-element.68, f32[1152]{0:T(1024)S(1)} %get-tuple-element.55, f32[1152]{0:T(1024)S(1)} %get-tuple-element.56, f32[128]{0:T(128)S(1)} %add_rsqrt_fusion.1, f32[128]{0:T(128)S(1)} %broadcast_multiply_fusion.1), kind=kOutput, calls=%fused_computation.20 | convolution fusion | flops 1020542976 | bytes 9152512 | tf_op jit(solution)/shard_map/dot_general | solution.py:42
  317.2 4.2 %reshape.164 = bf16[2,64,3,16,72]{4,3,2,1,0:T(8,128)(2,1)S(1)} reshape(bf16[128,3456]{1,0:T(8,128)(2,1)} %fusion.19) | data formatting | bytes 1769472 | tf_op jit(solution)/shard_map/reshape | solution.py:111
  321.4 3.6 copy.101
  324.9 3.7 reshape.165
  328.7 2.8 copy.103
  331.4 3.4 reshape.185
  334.8 19.7 %all_to_all.54 = bf16[8,2,27648]{2,1,0:T(2,128)(2,1)} all-to-all(bf16[8,2,27648]{2,1,0:T(2,128)(2,1)} %reshape.185), channel_id=1, replica_groups=mesh['frame'=8,'space'=32] {'frame'}, dimensions={0} | all-to-all | bytes 1769472 | tf_op jit(solution)/shard_map/all_to_all | solution.py:113
  354.5 4.0 %reshape.186 = bf16[1024,3,144]{2,1,0:T(4,128)(2,1)S(1)} reshape(bf16[8,2,27648]{2,1,0:T(2,128)(2,1)} %all_to_all.54) | data formatting | bytes 1769472
  358.5 2.5 copy.97
  367.5 10.8 %all_to_all.55 = bf16[128,8,144]{0,2,1:T(8,128)(2,1)S(1)} all-to-all(bf16[128,8,144]{0,2,1:T(8,128)(2,1)S(1)} %bitcast.100), channel_id=1, replica_groups=mesh['frame'=8,'space'=32] {'frame'}, dimensions={1} | all-to-all | bytes 589824 | tf_op jit(solution)/shard_map/all_to_all | solution.py:126
  379.5 3.1 fusion.40
  (92 shorter events, 52.6 us)
Async XLA Ops:
  6.5 1.2 copy-start
  6.5 5.6 %copy-start.6 = (bf16[36,1152]{1,0:T(8,128)(2,1)S(1)}, bf16[36,1152]{1,0:T(8,128)(2,1)}, u32[]{:S(2)}) copy-start(bf16[36,1152]{1,0:T(8,128)(2,1)} %param.21) | copy-start | bytes 248836
  6.5 6.5 %copy-start.2 = (bf16[2,64,1152]{2,1,0:T(8,128)(2,1)S(1)}, bf16[2,64,1152]{2,1,0:T(8,128)(2,1)}, u32[]{:S(2)}) copy-start(bf16[2,64,1152]{2,1,0:T(8,128)(2,1)} %param.12) | copy-start | bytes 884740
  6.5 7.1 %copy-start.7 = (f32[6,1152]{1,0:T(8,128)S(1)}, f32[6,1152]{1,0:T(8,128)}, u32[]{:S(2)}) copy-start(f32[6,1152]{1,0:T(8,128)} %param.13) | copy-start | bytes 82948
  6.5 168.0 %all-gather.3.cloned.1.call-start = ((), (), s32[]{:S(2)}) async-start(), calls=%async_computation.4 | async-start | bytes 29061120 | tf_op jit(solution)/shard_map/all_gather | solution.py:68
  12.1 0.9 copy-start.3
  218.2 36.9 %all-to-all-start = ((bf16[3,32,4608]{2,0,1:T(4,128)(2,1)}), bf16[3,32,4608]{2,0,1:T(4,128)(2,1)S(1)}, u32[]{:S(2)}, u32[]{:S(2)}) async-start(bf16[3,32,4608]{2,0,1:T(4,128)(2,1)} %copy.76), calls=%async_computation | async-start | bytes 2359296 | tf_op jit(solution)/shard_map/all_to_all | solution.py:80
  274.6 10.2 %slice-start = ((bf16[1152,10968]{1,0:T(8,128)(2,1)}), bf16[1152,600]{1,0:T(8,128)(2,1)S(1)}, s32[]{:S(2)}) async-start(bf16[1152,10968]{1,0:T(8,128)(2,1)} %reshape.172), calls=%async_computation.5 | async-start | bytes 2949120 | tf_op jit(solution)/shard_map/slice | solution.py:74
  278.3 18.8 %all-to-all-start.1 = ((bf16[32,2,2304]{2,1,0:T(2,128)(2,1)}), bf16[32,2,2304]{2,1,0:T(2,128)(2,1)S(1)}, u32[]{:S(2)}, u32[]{:S(2)}) async-start(bf16[32,2,2304]{2,1,0:T(2,128)(2,1)} %reshape.183), calls=%async_computation.1 | async-start | bytes 589824 | tf_op jit(solution)/shard_map/all_to_all | solution.py:84
  303.5 2.7 copy-start.5
  305.9 2.8 copy-start.4
  378.9 3.7 copy-start.1
Sparse Core Ops, SparseCore 0:
  13.2 161.3 all-gather.2

commit v2 on v0

v2 whole, which is shorter than its diff:
```python
import functools
import math

import jax
import jax.numpy as jnp
from jax import lax
from jax.experimental import pallas as pl
from jax.experimental.pallas import tpu as pltpu
from jax.sharding import PartitionSpec as P

D = 1152
HEADS = 16
HD = 72
ROWS = 36
HALF = 576
TROWS = 40
TEXT = 8 * TROWS
CA = 384
CB = 512
MESH = pl.DeviceIdType.MESH
BF = jnp.bfloat16
F32 = jnp.float32
SCALE = 1.0 / math.sqrt(HD)
LOG2E = 1.4426950408889634
NSEM = 256


def modulate(values, shift, gain):
    row_mean = jnp.mean(values, axis=-1, keepdims=True)
    centred = values - row_mean
    variance = jnp.mean(centred * centred, axis=-1, keepdims=True)
    return (centred * lax.rsqrt(variance + 1e-06) * (1.0 + gain) + shift).astype(BF)


def nt(left, right):
    return lax.dot_general(left, right, (((1,), (1,)), ((), ())), preferred_element_type=F32)


def mm(left, right):
    return jnp.dot(left, right, preferred_element_type=F32)


def where_tile(tile):
    if tile < 16:
        return 0, tile // 2, 128 * (tile % 2)
    if tile < 24:
        return 0, tile - 16, 256
    return 1, (tile - 24) // 4, 128 * ((tile - 24) % 4)


def runs(first, count):
    found = []
    for tile in range(first, first + count):
        buf, part, col = where_tile(tile)
        if found:
            at, b, p, c, w = found[-1]
            if (b, p, c + w) == (buf, part, col):
                found[-1] = (at, b, p, c, w + 128)
                continue
        found.append((128 * (tile - first), buf, part, col, 128))
    return found


def kernel(
    latent, mod, wsp, wa, wb, tx, bias, out,
    nb, tok, res, s0, wqk, wvt, qb, kb, vt, scores, ot, oi,
    za, zb, ga, gb, gt, acc, xb, qt, at, ar, rs, rr, ssem, rsem,
):
    fr = lax.axis_index("frame")
    sp = lax.axis_index("space")
    y, xh = fr // 2, fr % 2
    xl, z, c = sp // 16, (sp // 2) % 8, sp % 2
    x = 2 * xh + xl
    oc = 1 - c

    def dev(y_, x_, z_, c_):
        return (y_ * 2 + x_ // 2, (x_ % 2) * 16 + z_ * 2 + c_)

    partner = dev(y, x, z, oc)
    zn = [dev(y, x, (z + 1) % 8, c), dev(y, x, (z + 7) % 8, c)]
    xn = [dev(y, (x + 1) % 4, z, c), dev(y, (x + 3) % 4, z, c)]
    xmate = dev(y, 2 * xh + (1 - xl), z, c)
    yn = [dev((y + d) % 4, x, z, c) for d in (1, 3, 2)]

    ids = [0]
    started = []

    def reserve(n):
        first = ids[0]
        ids[0] += n
        return first

    def send(src, dst, target):
        i = reserve(1)
        copy = pltpu.make_async_remote_copy(
            src_ref=src, dst_ref=dst, send_sem=ssem.at[i], recv_sem=rsem.at[i],
            device_id=target, device_id_type=MESH,
        )
        copy.start()
        started.append(copy)
        return copy

    barrier = pltpu.get_barrier_semaphore()
    for i in range(1, 32):
        pl.semaphore_signal(barrier, inc=1, device_id=(fr, (sp + i) % 32), device_id_type=MESH)
    for i in range(1, 8):
        for core in range(2):
            pl.semaphore_signal(
                barrier, inc=1, device_id=((fr + i) % 8, xl * 16 + z * 2 + core), device_id_type=MESH
            )
    pl.semaphore_signal(
        barrier, inc=1, device_id=dev(y, 2 * (1 - xh) + (1 - xl), z, c), device_id_type=MESH
    )

    for i in range(2):
        nb[i] = modulate(latent[i].astype(F32), mod[0:1], mod[1:2])
    tok[z, xl, c] = nb[xl]
    res[c] = latent[c]
    za[z, c] = wa[c]
    zb[z, c] = wb[c]
    part = 2 * y + c
    gt[part, xl, z, c] = tx[c]
    s0[xl, z, c] = wsp[2 * z + c]
    pl.semaphore_wait(barrier, 46)

    init_a = send(wa.at[oc], za.at[z, c], partner)
    init_t = send(tx.at[oc], gt.at[2 * y + oc, xl, z, c], partner)
    s_in = [send(wsp.at[2 * z + oc], s0.at[xl, z, c], partner)]
    tok_x = send(nb.at[1 - xl], tok.at[z, xl, c], xmate)
    init_b = send(wb.at[oc], zb.at[z, c], partner)
    res_in = send(latent.at[oc], res.at[c], partner)
    for d in (1, 7, 2, 6, 3, 5, 4):
        zt = (z + d) % 8
        s_in.append(send(wsp.at[2 * zt + c], s0.at[xl, z, c], dev(y, x, zt, c)))
        s_in.append(send(wsp.at[2 * zt + oc], s0.at[xl, z, c], dev(y, x, zt, oc)))

    def block(step, way):
        return (z + (8 - step if way == 0 else step)) % 8

    class Ring:
        def __init__(self, whole, halves):
            self.whole, self.halves, self.copies = whole, halves, {}

        def go(self, step):
            for way in range(2):
                b = block(step, way)
                ref = self.whole(b) if step < 3 else self.halves(b, way)
                self.copies[step, way] = send(ref, ref, zn[way])

        def come(self, step):
            for way in range(2):
                self.copies[step - 1, way].wait_recv()

    ring_a = Ring(lambda b: za.at[b], lambda b, h: za.at[b, h])
    ring_b = Ring(lambda b: zb.at[b], lambda b, h: zb.at[b, h])
    ring_t = Ring(lambda b: gt.at[part, xl, b], lambda b, h: gt.at[part, xl, b, h])
    ring_0 = Ring(lambda b: tok.at[b, xl, c], None)
    ring_1 = Ring(lambda b: tok.at[b, 1 - xl, c], None)
    tok_core = {}

    def tok_ring(ring, sub, step):
        if step < 3:
            ring.go(step)
        else:
            b = block(3, 0 if sub == 0 else 1)
            way = 0 if sub == 0 else 1
            ref = tok.at[b, xl if sub == 0 else 1 - xl, c]
            ring.copies[3, way] = send(ref, ref, zn[way])

    def tok_share(b, lo, key):
        ref = tok.at[b, lo, c]
        tok_core[key] = send(ref, ref, partner)

    init_a.wait_recv()
    ring_a.go(0)
    ring_0.go(0)
    tok_share(z, xl, (0, 0, 0))
    init_t.wait_recv()
    ring_t.go(0)
    tok_x.wait_recv()
    ring_1.go(0)
    tok_share(z, 1 - xl, (0, 0, 1))
    init_b.wait_recv()
    ring_b.go(0)

    def tok_step(step):
        for way in range(2):
            for sub, ring in ((0, ring_0), (1, ring_1)):
                ring.copies[step - 1, way].wait_recv()
        if step < 4:
            tok_ring(ring_0, 0, step)
            tok_ring(ring_1, 1, step)
        for way in range(2):
            for sub in range(2):
                tok_share(block(step, way), xl if sub == 0 else 1 - xl, (step, way, sub))

    def tok_last():
        ring_0.copies[3, 0].wait_recv()
        ring_1.copies[3, 1].wait_recv()
        tok_share(block(4, 0), xl, (4, 0, 0))
        tok_share(block(4, 0), 1 - xl, (4, 0, 1))

    def tok_ready(step, way):
        for sub in range(2):
            tok_core[step, way, sub].wait_recv()

    class Spread:
        def __init__(self, lo_rows, half_rows, first, second):
            self.lo_rows, self.half_rows = lo_rows, half_rows
            self.x_copies, self.core_copies = [], []

        def start(self):
            mine = self.lo_rows(part, xl)
            self.y_copies = [send(mine, mine, t) for t in yn]
            self.spread(y)

        def spread(self, yq):
            e = 2 * yq + c
            xs = []
            for way in range(2):
                ref = self.half_rows(e, xl, way)
                xs.append(send(ref, ref, xn[way]))
            self.x_copies.append((e, xs))
            ref = self.lo_rows(e, xl)
            self.core_copies.append(send(ref, ref, partner))

        def y_come(self, k):
            self.y_copies[k].wait_recv()
            self.spread((y + 4 - (1, 3, 2)[k]) % 4)

        def x_come(self, k):
            e, xs = self.x_copies[k]
            for way in range(2):
                xs[way].wait_recv()
                ref = self.half_rows(e, 1 - xl, way)
                self.core_copies.append(send(ref, ref, partner))

        def finish(self):
            for copy in self.core_copies:
                copy.wait_recv()

    def rows_of(buf):
        def lo_rows(e, lo):
            return buf.at[e, pl.ds(pl.multiple_of(lo * HALF, HALF), HALF)]

        def half_rows(e, lo, way):
            return buf.at[e, pl.ds(pl.multiple_of(lo * HALF + way * (HALF // 2), HALF // 2), HALF // 2)]

        return lo_rows, half_rows

    spread_a = Spread(*rows_of(ga), 0, 0)
    spread_b = Spread(*rows_of(gb), 0, 0)
    spread_t = Spread(
        lambda e, lo: gt.at[e, lo], lambda e, lo, way: gt.at[e, lo, pl.ds(4 * way, 4)], 0, 0
    )

    def compact(zref, gref):
        for k in range(4):
            rows = jnp.concatenate([zref[2 * k + i // 2, i % 2] for i in range(4)], axis=0)
            gref[part, pl.ds(pl.multiple_of(xl * HALF + 144 * k, 144), 144)] = rows

    def qkv(b):
        rows = tok[b].reshape(256, D)
        qk = mm(rows, wqk[...]).astype(BF)
        qb[b] = qk[:, :128]
        kb[b] = qk[:, 128:]
        v = nt(wvt[...], rows)
        ones = lax.broadcasted_iota(jnp.int32, v.shape, 0) == HD
        vt[b] = jnp.where(ones, 1.0, v).astype(BF)

    for step in (1, 2):
        ring_a.come(step)
        ring_a.go(step)
        ring_t.come(step)
        ring_t.go(step)
    for copy in s_in:
        copy.wait_recv()
    s_x = [
        send(s0.at[xl, pl.ds(4 * way, 4)], s0.at[xl, pl.ds(4 * way, 4)], xn[way]) for way in range(2)
    ]
    tok_step(1)
    ring_b.come(1)
    ring_b.go(1)
    ring_a.come(3)
    ring_a.go(3)
    ring_t.come(3)
    ring_t.go(3)
    for copy in s_x:
        copy.wait_recv()
    joined = s0[...].reshape(32 * ROWS, 256).astype(F32)
    blank = jnp.zeros((D, 128 - HD), F32)
    wqk[...] = jnp.concatenate([joined[:, :HD], blank, joined[:, HD : 2 * HD], blank], axis=1).astype(BF)
    wvt[...] = jnp.concatenate([joined[:, 2 * HD : 3 * HD], blank], axis=1).T[:80].astype(BF)
    ring_a.come(4)
    compact(za, ga)
    spread_a.start()
    ring_t.come(4)
    spread_t.start()
    tok_ready(0, 0)
    qkv(z)
    ring_b.come(2)
    ring_b.go(2)
    tok_step(2)
    for way in range(2):
        tok_ready(1, way)
        qkv(block(1, way))
    ring_b.come(3)
    ring_b.go(3)
    spread_a.y_come(0)
    spread_a.y_come(1)
    tok_step(3)
    ring_b.come(4)
    compact(zb, gb)
    spread_b.start()
    for way in range(2):
        tok_ready(2, way)
        qkv(block(2, way))
    spread_t.y_come(0)
    spread_t.y_come(1)
    spread_a.y_come(2)
    spread_a.x_come(0)
    spread_t.y_come(2)
    spread_t.x_come(0)
    tok_last()
    for way in range(2):
        tok_ready(3, way)
        qkv(block(3, way))
    tok_ready(4, 0)
    qkv(block(4, 0))

    oi_id = reserve(16)
    head = 2 * z + c

    def attn_copy(i, lo):
        zt = (z + 1 + i) % 8
        i_send = oi_id + 2 * i + lo
        return (
            pltpu.make_async_remote_copy(
                src_ref=ot.at[zt, lo], dst_ref=oi.at[head],
                send_sem=ssem.at[i_send], recv_sem=rsem.at[oi_id + head],
                device_id=(fr, lo * 16 + zt * 2 + xl), device_id_type=MESH,
            ),
            pltpu.make_async_copy(ot.at[zt, lo], oi.at[head], rsem.at[oi_id + head]),
            jnp.logical_and(zt == z, jnp.logical_and(xl == lo, c == xl)),
        )

    def tile(i, carry):
        zt = (z + 1 + i) % 8
        queries = qb[zt]
        top = jnp.full((1, 256), -jnp.inf, F32)
        for k in range(4):
            s = nt(kb[2 * k : 2 * k + 2].reshape(512, 128), queries)
            scores[512 * k : 512 * (k + 1)] = s
            top = jnp.maximum(top, jnp.max(s, axis=0, keepdims=True))
        top = top * (SCALE * LOG2E)
        total = jnp.zeros((80, 256), F32)
        for k in range(8):
            p = jnp.exp2(scores[256 * k : 256 * (k + 1)] * (SCALE * LOG2E) - top)
            total = total + mm(vt[k], p.astype(BF))
        mixed = (total[:HD] / total[HD : HD + 1]).astype(BF)
        for lo in range(2):
            ot[zt, lo] = mixed[:, 128 * lo : 128 * (lo + 1)]
            far, near, own = attn_copy(i, lo)

            @pl.when(own)
            def _():
                near.start()

            @pl.when(jnp.logical_not(own))
            def _():
                far.start()

        return carry

    lax.fori_loop(0, 4, tile, 0)
    spread_b.y_come(0)
    spread_b.y_come(1)
    spread_a.x_come(1)
    spread_a.x_come(2)
    spread_t.x_come(1)
    spread_t.x_come(2)
    lax.fori_loop(4, 8, tile, 0)
    spread_a.x_come(3)
    spread_t.x_come(3)
    spread_b.x_come(0)
    for i in range(HEADS):
        pltpu.make_async_copy(ot.at[0, 0], oi.at[i], rsem.at[oi_id + i]).wait()

    bufs = (ga, gb)

    def project(rows, first, count, put):
        for at_col, buf, e, col, width in runs(first, count):
            put(at_col, width, mm(rows, bufs[buf][e, :, col : col + width]))

    def put_acc(at_col, width, value):
        acc[:, at_col : at_col + width] = value

    spread_a.finish()
    rows = oi[...].reshape(D, 128).T
    project(rows, 0, 9, put_acc)
    res_in.wait_recv()
    own = res[...].reshape(128, D).astype(F32)
    after_space = (own + mod[2:3] * acc[...]).astype(BF)

    def put_qt(at_col, width, value):
        qt[:, at_col : at_col + width] = value.astype(BF)

    project(after_space, 9, 9, put_qt)
    qt[:, D : D + 128] = jnp.zeros((128, 128), BF)
    spread_b.y_come(2)
    spread_b.x_come(1)
    spread_t.finish()
    mixed = []
    for h in range(HEADS):
        keys = gt[:, 0, h // 2, h % 2].reshape(TEXT, 128)
        values = gt[:, 1, h // 2, h % 2].reshape(TEXT, 128)
        s = nt(qt[:, HD * h : HD * h + 128], keys) * SCALE + bias[...]
        p = jnp.exp(s - jnp.max(s, axis=-1, keepdims=True))
        w = (p / jnp.sum(p, axis=-1, keepdims=True)).astype(BF)
        mixed.append(mm(w, values)[:, :HD])
    crossed = jnp.concatenate(mixed, axis=1).astype(BF)
    after_text = (after_space.astype(F32) + crossed.astype(F32)).astype(BF)
    at[...] = after_text.reshape(16, 8, D)

    me = 2 * fr + c
    ar[me] = at[me]
    time_in = []
    for k in range(1, 16):
        p = (me + k) % 16
        time_in.append(send(at.at[p], ar.at[me], (p // 2, xl * 16 + z * 2 + p % 2)))
    spread_b.x_come(2)
    for copy in time_in:
        copy.wait_recv()
    tokens = ar[...].reshape(128, D).astype(F32)
    xb[...] = modulate(tokens, mod[3:4], mod[4:5])
    spread_b.x_come(3)
    spread_b.finish()
    project(xb[...], 18, 27, put_qt)
    qt[:, 3 * D :] = jnp.zeros((128, 128), BF)
    lanes = lax.broadcasted_iota(jnp.int32, (128, 128), 1)
    subs = lax.broadcasted_iota(jnp.int32, (128, 128), 0)
    same = (lanes % 8) == (subs % 8)
    real = lanes < HD
    mixed = []
    for h in range(HEADS):
        q = qt[:, HD * h : HD * h + 128]
        k = jnp.where(real, qt[:, D + HD * h : D + HD * h + 128], 0)
        v = qt[:, 2 * D + HD * h : 2 * D + HD * h + 128]
        s = jnp.where(same, nt(q, k) * SCALE, -jnp.inf)
        p = jnp.exp(s - jnp.max(s, axis=-1, keepdims=True))
        w = (p / jnp.sum(p, axis=-1, keepdims=True)).astype(BF)
        mixed.append(mm(w, v)[:, :HD])
    temporal = jnp.concatenate(mixed, axis=1).astype(BF)
    project(temporal, 45, 9, put_acc)
    result = (ar[...].reshape(128, D).astype(F32) + mod[5:6] * acc[...]).astype(BF)
    rs[...] = result.reshape(8, 2, 8, D)

    back_id = reserve(8)
    slot = (2 * fr + c) % 8
    back = []
    for k in range(8):
        ft = (fr + k) % 8
        far = pltpu.make_async_remote_copy(
            src_ref=rs.at[ft], dst_ref=rr.at[slot],
            send_sem=ssem.at[back_id + k], recv_sem=rsem.at[back_id + slot],
            device_id=(ft, xl * 16 + z * 2 + fr // 4), device_id_type=MESH,
        )
        back.append(far)
        if k == 0:
            near = pltpu.make_async_copy(rs.at[ft], rr.at[slot], rsem.at[back_id + slot])

            @pl.when(c == fr // 4)
            def _():
                near.start()

            @pl.when(c != fr // 4)
            def _():
                far.start()
        else:
            far.start()
    for k in range(8):
        pltpu.make_async_copy(rs.at[0], rr.at[k], rsem.at[back_id + k]).wait()
    for i in range(2):
        out[i] = rr[:, i].reshape(64, D)

    for copy in started:
        copy.wait_send()
    for i in range(8):
        for lo in range(2):
            far, near, own = attn_copy(i, lo)

            @pl.when(jnp.logical_not(own))
            def _():
                far.wait_send()

    @pl.when(c != fr // 4)
    def _():
        back[0].wait_send()

    for k in range(1, 8):
        back[k].wait_send()


def local(
    latent, modulation, w_spatial, w_spatial_out, caption_states, w_text_kv, w_cross_q, text_len,
    w_time, w_time_out,
):
    y = lax.axis_index("frame") // 2
    wsp = w_spatial.reshape(ROWS, 3, HEADS, HD).transpose(2, 0, 1, 3).reshape(HEADS, ROWS, 3 * HD)
    wsp = jnp.pad(wsp, ((0, 0), (0, 0), (0, 256 - 3 * HD)))
    joined = jnp.concatenate(
        [w_spatial_out, w_cross_q, w_time, w_time_out, jnp.zeros((ROWS, 256), BF)], axis=1
    )

    def cut(first, width):
        piece = lax.dynamic_slice(joined, (0, first + 2 * width * y), (ROWS, 2 * width))
        return piece.reshape(ROWS, 2, width).transpose(1, 0, 2)

    wa = jnp.concatenate([cut(0, 256), cut(2048, 128)], axis=2)
    wb = cut(3072, CB)
    text_count = caption_states.shape[0]
    caption = jnp.pad(caption_states, ((0, TEXT - text_count), (0, 0)))
    caption = lax.dynamic_slice(caption, (2 * TROWS * y, 0), (2 * TROWS, D))
    text = jnp.dot(caption, w_text_kv, preferred_element_type=F32).astype(BF)
    text = jnp.pad(text, ((0, 0), (0, 128 - HD))).reshape(2, TROWS, 128)
    bias = jnp.where(jnp.arange(TEXT) < text_len[0], 0.0, -jnp.inf).astype(F32)[None, :]

    vmem = pl.BlockSpec(memory_space=pltpu.VMEM)
    return pl.pallas_call(
        kernel,
        out_shape=jax.ShapeDtypeStruct(latent.shape, BF),
        in_specs=[vmem] * 7,
        out_specs=vmem,
        scratch_shapes=[
            pltpu.VMEM((2, 64, D), BF),
            pltpu.VMEM((8, 2, 2, 64, D), BF),
            pltpu.VMEM((2, 64, D), BF),
            pltpu.VMEM((2, 8, 2, ROWS, 256), BF),
            pltpu.VMEM((D, 256), BF),
            pltpu.VMEM((80, D), BF),
            pltpu.VMEM((8, 256, 128), BF),
            pltpu.VMEM((8, 256, 128), BF),
            pltpu.VMEM((8, 80, 256), BF),
            pltpu.VMEM((2048, 256), F32),
            pltpu.VMEM((8, 2, HD, 128), BF),
            pltpu.VMEM((HEADS, HD, 128), BF),
            pltpu.VMEM((8, 2, ROWS, CA), BF),
            pltpu.VMEM((8, 2, ROWS, CB), BF),
            pltpu.VMEM((8, D, CA), BF),
            pltpu.VMEM((8, D, CB), BF),
            pltpu.VMEM((8, 2, 8, 2, TROWS, 128), BF),
            pltpu.VMEM((128, D), F32),
            pltpu.VMEM((128, D), BF),
            pltpu.VMEM((128, 3 * D + 128), BF),
            pltpu.VMEM((16, 8, D), BF),
            pltpu.VMEM((16, 8, D), BF),
            pltpu.VMEM((8, 2, 8, D), BF),
            pltpu.VMEM((8, 2, 8, D), BF),
            pltpu.SemaphoreType.DMA((NSEM,)),
            pltpu.SemaphoreType.DMA((NSEM,)),
        ],
        compiler_params=pltpu.CompilerParams(
            collective_id=0, has_side_effects=True, vmem_limit_bytes=60 << 20
        ),
        name="block",
    )(latent, modulation, wsp, wa, wb, text, bias)


def solution(mesh):
    placed = (
        P("frame", "space", None),
        P(),
        P("space", None),
        P("space", None),
        P(),
        P(None, "space"),
        P("space", None),
        P(),
        P("space", None),
        P("space", None),
    )
    return jax.shard_map(
        local, mesh=mesh, in_specs=placed, out_specs=P("frame", "space", None), check_vma=False
    )
```

time: 489 us -> 148 us (0.30); the launches traced: 481 us -> 147 us
  waiting for transfers between devices: 283 us -> 0 us
  Pallas kernels: 0 us -> 137 us
  local copies, waits for them, and re-layouts: 105 us -> 8.16 us
  matrix products: 29.9 us -> 0.2 us
  blocking collectives: 21.8 us -> 0 us
  starting transfers between devices: 15.8 us -> 0 us
  between operations: 14.9 us -> 0.79 us
  other arithmetic: 10.7 us -> 1.23 us
    all_gather x6 -> x0, waiting for transfers between devices: 244 us -> none  [the longest x5 244 us: project(): lax.all_gather(weight, 'space', axis=0, tiled=True)]
    pallas_call x0 -> x1, Pallas kernels: none -> 137 us  [local(): pl.pallas_call(kernel, out_shape=jax.ShapeDtypeStruct(latent.shape, BF),...]
    unnamed x26 -> x16, local copies, waits for them, and re-layouts: 48.4 us -> 4.58 us
    all_to_all x3 -> x0, waiting for transfers between devices: 36.6 us -> none  [the longest x1 32.4 us: local(): lax.all_to_all(sectioned, 'space', split_axis=1, concat_axis=2, tiled=True)]
    reshape x13 -> x10, local copies, waits for them, and re-layouts: 31.4 us -> 2.16 us  [the longest x4 1.42 us: local(): w_spatial.reshape(ROWS, 3, HEADS, HD).transpose(2, 0, 1, 3)]
    dot_general x17 -> x1, matrix products: 26.7 us -> 0.2 us  [local(): text = jnp.dot(caption, w_text_kv, preferred_element_type=F32).astype(BF)]
    all_to_all x1 -> x0, blocking collectives: 21.8 us -> none  [local(): lax.all_to_all(sectioned_t, 'frame', split_axis=1, concat_axis=2, tiled=T...]
    all_to_all x3 -> x0, starting transfers between devices: 15.4 us -> none  [the longest x1 6.27 us: local(): lax.all_to_all(sectioned, 'space', split_axis=1, concat_axis=2, tiled=True)]
  transfers between devices with their start and end apart: 9 -> 0, of which waited for: 6 -> 0; matrix products, arithmetic and copies ran while one was open for 28% -> 0% of each run, Pallas kernels for 0% -> 0%
where the time goes in v2:
time: 148 us; the launch traced here: 147 us
  Pallas kernels  137 us (93%)
  local copies, waits for them, and re-layouts  8.16 us (6%)
    pallas_call x1, Pallas kernels, local(): pl.pallas_call(kernel, out_shape=jax.ShapeDtypeStruct(latent.shape, BF),...  137 us
    unnamed x16, local copies, waits for them, and re-layouts  4.58 us

profile of v2, /device:TPU:1, one launch (start us, length us, event | category | flops | bytes accessed | tf_op | source)
XLA Modules:
  0.0 147.4 jit_solution(13504935590707332397)
XLA Ops:
  0.0 0.0 copy-start
  0.0 0.0 copy-start.2
  0.0 1.0 constant_dynamic-update-slice_fusion.4
  1.0 0.9 constant_dynamic-update-slice_fusion.3
  1.9 0.0 copy-done.2
  1.9 0.0 copy-start.4
  1.9 0.8 copy-done.4
  2.8 0.0 copy-start.1
  2.9 0.6 pad_maximum_fusion.wa
  3.6 0.6 copy.25
  4.2 0.0 copy-done
  4.2 0.0 copy-done.1
  4.2 0.2 convolution_convert_fusion
  4.5 0.1 copy.19
  4.6 0.6 pad.14.clone
  5.2 0.0 copy-done.3
  5.2 0.8 reshape.28
  6.0 0.3 copy.24
  6.3 0.3 reshape.29
  6.6 0.1 copy.14
  6.7 0.8 pad.12.wsp
  8.1 0.6 compare_select_fusion.bias
  8.7 137.0 %block.1 = bf16[2,64,1152]{2,1,0:T(8,128)(2,1)} custom-call(bf16[2,64,1152]{2,1,0:T(8,128)(2,1)} %latent.1, f32[6,1152]{1,0:T(8,128)} %mod.1, bf16[16,36,256]{2,1,0:T(8,128)(2,1)} %pad.12.wsp, bf16[2,36,384]{2,1,0:T(8,128)(2,1)} %pad_maximum_fusion.wa, bf16[2,36,512]{2,1,0:T(8,128)(2,1)} %bitcast.19, bf16[2,40,128]{2,1,0:T(8,128)(2,1)} %bitcast.22, ...), custom_call_target="tpu_custom_call" | custom-call | tf_op jit(solution)/shard_map/block/pallas_call | solution.py:529
  145.7 1.7 %copy.34 = bf16[2,64,1152]{2,1,0:T(8,128)(2,1)} copy(bf16[2,64,1152]{2,1,0:T(8,128)(2,1)} %block.1) | data formatting | bytes 589824
  (12 shorter events, 0.2 us)
Async XLA Ops:
  0.0 4.2 %copy-start = (bf16[1152,72]{0,1:T(8,128)(2,1)S(1)}, bf16[1152,72]{0,1:T(8,128)(2,1)}, u32[]{:S(2)}) copy-start(bf16[1152,72]{0,1:T(8,128)(2,1)} %param.15) | copy-start | bytes 497668
  0.0 1.9 %copy-start.2 = (bf16[36,3456]{1,0:T(8,128)(2,1)S(1)}, bf16[36,3456]{1,0:T(8,128)(2,1)}, u32[]{:S(2)}) copy-start(bf16[36,3456]{1,0:T(8,128)(2,1)} %param.18) | copy-start | bytes 746500
  1.9 0.9 copy-start.4
  2.8 1.5 %copy-start.1 = (bf16[300,1152]{1,0:T(8,128)(2,1)S(1)}, bf16[300,1152]{1,0:T(8,128)(2,1)}, u32[]{:S(2)}) copy-start(bf16[300,1152]{1,0:T(8,128)(2,1)} %param.14) | copy-start | bytes 2073604
  4.2 1.0 copy-start.3

commit v3 on v2

--- a/solution.py
+++ b/solution.py
@@ -62,8 +62,8 @@
 
 
 def kernel(
-    latent, mod, wsp, wa, wb, tx, bias, out,
-    nb, tok, res, s0, wqk, wvt, qb, kb, vt, scores, ot, oi,
+    latent, mod, w_spatial, w_out, caption, w_text, w_cross, text_len, w_time, w_time_out, out,
+    wsp, wa, wb, tx, nb, tok, res, s0, wqk, wvt, qb, kb, vt, scores, ot, oi,
     za, zb, ga, gb, gt, acc, xb, qt, at, ar, rs, rr, ssem, rsem,
 ):
     fr = lax.axis_index("frame")
@@ -80,7 +80,7 @@
     zn = [dev(y, x, (z + 1) % 8, c), dev(y, x, (z + 7) % 8, c)]
     xn = [dev(y, (x + 1) % 4, z, c), dev(y, (x + 3) % 4, z, c)]
     xmate = dev(y, 2 * xh + (1 - xl), z, c)
-    yn = [dev((y + d) % 4, x, z, c) for d in (1, 3, 2)]
+    yn = [dev((y + d) % 4, x, z, c) for d in (1, 3)]
 
     ids = [0]
     started = []
@@ -112,27 +112,59 @@
         barrier, inc=1, device_id=dev(y, 2 * (1 - xh) + (1 - xl), z, c), device_id_type=MESH
     )
 
+    def tile_of(t):
+        for ref, first in ((w_out, 0), (w_cross, 9), (w_time, 18), (w_time_out, 45)):
+            if t - first < ref.shape[1] // 128:
+                return ref[:, 128 * (t - first) : 128 * (t - first + 1)]
+        return jnp.zeros((ROWS, 128), BF)
+
+    for quarter in range(4):
+
+        @pl.when(y == quarter)
+        def _():
+            for core in range(2):
+                e = 2 * quarter + core
+                for i, t in enumerate((2 * e, 2 * e + 1, 16 + e)):
+                    wa[core, :, 128 * i : 128 * (i + 1)] = tile_of(t)
+                for i in range(4):
+                    wb[core, :, 128 * i : 128 * (i + 1)] = tile_of(24 + 4 * e + i)
+            first = 2 * TROWS * quarter
+            count = min(2 * TROWS, caption.shape[0] - first)
+            text = nt(caption[first : first + count], w_text[...])
+            text = jnp.concatenate([text, jnp.zeros((count, 128 - HD), F32)], axis=1)
+            if count < 2 * TROWS:
+                text = jnp.concatenate([text, jnp.zeros((2 * TROWS - count, 128), F32)], axis=0)
+            tx[...] = text.astype(BF).reshape(2, TROWS, 128)
+
+    part = 2 * y + c
+    za[z, c] = wa[c]
+    zb[z, c] = wb[c]
+    gt[part, xl, z, c] = tx[c]
+
     for i in range(2):
         nb[i] = modulate(latent[i].astype(F32), mod[0:1], mod[1:2])
     tok[z, xl, c] = nb[xl]
     res[c] = latent[c]
-    za[z, c] = wa[c]
-    zb[z, c] = wb[c]
-    part = 2 * y + c
-    gt[part, xl, z, c] = tx[c]
+
+    for h in range(HEADS):
+        cols = [w_spatial[:, D * i + HD * h : D * i + HD * (h + 1)] for i in range(3)]
+        wsp[h] = jnp.concatenate(cols + [jnp.zeros((ROWS, 256 - 3 * HD), BF)], axis=1)
     s0[xl, z, c] = wsp[2 * z + c]
     pl.semaphore_wait(barrier, 46)
 
     init_a = send(wa.at[oc], za.at[z, c], partner)
     init_t = send(tx.at[oc], gt.at[2 * y + oc, xl, z, c], partner)
-    s_in = [send(wsp.at[2 * z + oc], s0.at[xl, z, c], partner)]
+    init_b = send(wb.at[oc], zb.at[z, c], partner)
     tok_x = send(nb.at[1 - xl], tok.at[z, xl, c], xmate)
-    init_b = send(wb.at[oc], zb.at[z, c], partner)
-    res_in = send(latent.at[oc], res.at[c], partner)
-    for d in (1, 7, 2, 6, 3, 5, 4):
-        zt = (z + d) % 8
-        s_in.append(send(wsp.at[2 * zt + c], s0.at[xl, z, c], dev(y, x, zt, c)))
-        s_in.append(send(wsp.at[2 * zt + oc], s0.at[xl, z, c], dev(y, x, zt, oc)))
+
+    s_in = []
+
+    def give_spatial(*offsets):
+        for d in offsets:
+            zt = (z + d) % 8
+            if d:
+                s_in.append(send(wsp.at[2 * zt + c], s0.at[xl, z, c], dev(y, x, zt, c)))
+            s_in.append(send(wsp.at[2 * zt + oc], s0.at[xl, z, c], dev(y, x, zt, oc)))
 
     def block(step, way):
         return (z + (8 - step if way == 0 else step)) % 8
@@ -170,18 +202,6 @@
     def tok_share(b, lo, key):
         ref = tok.at[b, lo, c]
         tok_core[key] = send(ref, ref, partner)
-
-    init_a.wait_recv()
-    ring_a.go(0)
-    ring_0.go(0)
-    tok_share(z, xl, (0, 0, 0))
-    init_t.wait_recv()
-    ring_t.go(0)
-    tok_x.wait_recv()
-    ring_1.go(0)
-    tok_share(z, 1 - xl, (0, 0, 1))
-    init_b.wait_recv()
-    ring_b.go(0)
 
     def tok_step(step):
         for way in range(2):
@@ -205,14 +225,19 @@
             tok_core[step, way, sub].wait_recv()
 
     class Spread:
-        def __init__(self, lo_rows, half_rows, first, second):
+        def __init__(self, lo_rows, half_rows):
             self.lo_rows, self.half_rows = lo_rows, half_rows
-            self.x_copies, self.core_copies = [], []
+            self.x_copies, self.core_copies, self.y_halves = [], [], []
 
         def start(self):
             mine = self.lo_rows(part, xl)
             self.y_copies = [send(mine, mine, t) for t in yn]
             self.spread(y)
+
+        def y_last(self):
+            for copy in self.y_halves:
+                copy.wait_recv()
+            self.spread((y + 2) % 4)
 
         def spread(self, yq):
             e = 2 * yq + c
@@ -226,7 +251,10 @@
 
         def y_come(self, k):
             self.y_copies[k].wait_recv()
-            self.spread((y + 4 - (1, 3, 2)[k]) % 4)
+            yq = (y + (3, 1)[k]) % 4
+            ref = self.half_rows(2 * yq + c, xl, k)
+            self.y_halves.append(send(ref, ref, yn[k]))
+            self.spread(yq)
 
         def x_come(self, k):
             e, xs = self.x_copies[k]
@@ -248,10 +276,10 @@
 
         return lo_rows, half_rows
 
-    spread_a = Spread(*rows_of(ga), 0, 0)
-    spread_b = Spread(*rows_of(gb), 0, 0)
+    spread_a = Spread(*rows_of(ga))
+    spread_b = Spread(*rows_of(gb))
     spread_t = Spread(
-        lambda e, lo: gt.at[e, lo], lambda e, lo, way: gt.at[e, lo, pl.ds(4 * way, 4)], 0, 0
+        lambda e, lo: gt.at[e, lo], lambda e, lo, way: gt.at[e, lo, pl.ds(4 * way, 4)]
     )
 
     def compact(zref, gref):
@@ -268,65 +296,75 @@
         ones = lax.broadcasted_iota(jnp.int32, v.shape, 0) == HD
         vt[b] = jnp.where(ones, 1.0, v).astype(BF)
 
-    for step in (1, 2):
-        ring_a.come(step)
-        ring_a.go(step)
-        ring_t.come(step)
-        ring_t.go(step)
+    rings = (ring_a, ring_t, ring_b)
+
+    def weight_step(step):
+        for ring in rings:
+            ring.come(step)
+            ring.go(step)
+
+    for copy, ring in zip((init_a, init_t, init_b), rings):
+        copy.wait_recv()
+        ring.go(0)
+    ring_0.go(0)
+    tok_share(z, xl, (0, 0, 0))
+    weight_step(1)
+    tok_x.wait_recv()
+    ring_1.go(0)
+    tok_share(z, 1 - xl, (0, 0, 1))
+    weight_step(2)
+    weight_step(3)
+    give_spatial(0, 1, 7, 2, 6, 3, 5, 4)
+    ring_a.come(4)
+    compact(za, ga)
+    spread_a.start()
+    ring_t.come(4)
+    spread_t.start()
+    ring_b.come(4)
+    compact(zb, gb)
+    spread_b.start()
+    res_in = send(latent.at[oc], res.at[c], partner)
+    tok_step(1)
     for copy in s_in:
         copy.wait_recv()
     s_x = [
         send(s0.at[xl, pl.ds(4 * way, 4)], s0.at[xl, pl.ds(4 * way, 4)], xn[way]) for way in range(2)
     ]
-    tok_step(1)
-    ring_b.come(1)
-    ring_b.go(1)
-    ring_a.come(3)
-    ring_a.go(3)
-    ring_t.come(3)
-    ring_t.go(3)
+    tok_step(2)
+    spread_a.y_come(0)
+    spread_a.y_come(1)
+    spread_a.x_come(0)
+    spread_t.y_come(0)
+    spread_t.y_come(1)
+    spread_t.x_come(0)
     for copy in s_x:
         copy.wait_recv()
     joined = s0[...].reshape(32 * ROWS, 256).astype(F32)
     blank = jnp.zeros((D, 128 - HD), F32)
     wqk[...] = jnp.concatenate([joined[:, :HD], blank, joined[:, HD : 2 * HD], blank], axis=1).astype(BF)
     wvt[...] = jnp.concatenate([joined[:, 2 * HD : 3 * HD], blank], axis=1).T[:80].astype(BF)
-    ring_a.come(4)
-    compact(za, ga)
-    spread_a.start()
-    ring_t.come(4)
-    spread_t.start()
     tok_ready(0, 0)
     qkv(z)
-    ring_b.come(2)
-    ring_b.go(2)
-    tok_step(2)
     for way in range(2):
         tok_ready(1, way)
         qkv(block(1, way))
-    ring_b.come(3)
-    ring_b.go(3)
-    spread_a.y_come(0)
-    spread_a.y_come(1)
     tok_step(3)
-    ring_b.come(4)
-    compact(zb, gb)
-    spread_b.start()
     for way in range(2):
         tok_ready(2, way)
         qkv(block(2, way))
-    spread_t.y_come(0)
-    spread_t.y_come(1)
-    spread_a.y_come(2)
-    spread_a.x_come(0)
-    spread_t.y_come(2)
-    spread_t.x_come(0)
+    spread_a.y_last()
+    spread_t.y_last()
+    spread_b.x_come(0)
     tok_last()
     for way in range(2):
         tok_ready(3, way)
         qkv(block(3, way))
     tok_ready(4, 0)
     qkv(block(4, 0))
+    spread_a.x_come(1)
+    spread_a.x_come(2)
+    spread_t.x_come(1)
+    spread_t.x_come(2)
 
     oi_id = reserve(16)
     head = 2 * z + c
@@ -372,17 +410,15 @@
 
         return carry
 
-    lax.fori_loop(0, 4, tile, 0)
+    lax.fori_loop(0, 2, tile, 0)
     spread_b.y_come(0)
     spread_b.y_come(1)
-    spread_a.x_come(1)
-    spread_a.x_come(2)
-    spread_t.x_come(1)
-    spread_t.x_come(2)
-    lax.fori_loop(4, 8, tile, 0)
+    lax.fori_loop(2, 5, tile, 0)
     spread_a.x_come(3)
     spread_t.x_come(3)
-    spread_b.x_come(0)
+    lax.fori_loop(5, 8, tile, 0)
+    spread_b.y_last()
+    spread_b.x_come(1)
     for i in range(HEADS):
         pltpu.make_async_copy(ot.at[0, 0], oi.at[i], rsem.at[oi_id + i]).wait()
 
@@ -407,14 +443,15 @@
 
     project(after_space, 9, 9, put_qt)
     qt[:, D : D + 128] = jnp.zeros((128, 128), BF)
-    spread_b.y_come(2)
-    spread_b.x_come(1)
+    spread_b.x_come(2)
     spread_t.finish()
+    valid = lax.broadcasted_iota(jnp.int32, (128, TEXT), 1) < text_len[0]
     mixed = []
     for h in range(HEADS):
         keys = gt[:, 0, h // 2, h % 2].reshape(TEXT, 128)
         values = gt[:, 1, h // 2, h % 2].reshape(TEXT, 128)
-        s = nt(qt[:, HD * h : HD * h + 128], keys) * SCALE + bias[...]
+        s = nt(qt[:, HD * h : HD * h + 128], keys) * SCALE
+        s = jnp.where(valid, s, -jnp.inf)
         p = jnp.exp(s - jnp.max(s, axis=-1, keepdims=True))
         w = (p / jnp.sum(p, axis=-1, keepdims=True)).astype(BF)
         mixed.append(mm(w, values)[:, :HD])
@@ -428,7 +465,6 @@
     for k in range(1, 16):
         p = (me + k) % 16
         time_in.append(send(at.at[p], ar.at[me], (p // 2, xl * 16 + z * 2 + p % 2)))
-    spread_b.x_come(2)
     for copy in time_in:
         copy.wait_recv()
     tokens = ar[...].reshape(128, D).astype(F32)
@@ -505,33 +541,17 @@
     latent, modulation, w_spatial, w_spatial_out, caption_states, w_text_kv, w_cross_q, text_len,
     w_time, w_time_out,
 ):
-    y = lax.axis_index("frame") // 2
-    wsp = w_spatial.reshape(ROWS, 3, HEADS, HD).transpose(2, 0, 1, 3).reshape(HEADS, ROWS, 3 * HD)
-    wsp = jnp.pad(wsp, ((0, 0), (0, 0), (0, 256 - 3 * HD)))
-    joined = jnp.concatenate(
-        [w_spatial_out, w_cross_q, w_time, w_time_out, jnp.zeros((ROWS, 256), BF)], axis=1
-    )
-
-    def cut(first, width):
-        piece = lax.dynamic_slice(joined, (0, first + 2 * width * y), (ROWS, 2 * width))
-        return piece.reshape(ROWS, 2, width).transpose(1, 0, 2)
-
-    wa = jnp.concatenate([cut(0, 256), cut(2048, 128)], axis=2)
-    wb = cut(3072, CB)
-    text_count = caption_states.shape[0]
-    caption = jnp.pad(caption_states, ((0, TEXT - text_count), (0, 0)))
-    caption = lax.dynamic_slice(caption, (2 * TROWS * y, 0), (2 * TROWS, D))
-    text = jnp.dot(caption, w_text_kv, preferred_element_type=F32).astype(BF)
-    text = jnp.pad(text, ((0, 0), (0, 128 - HD))).reshape(2, TROWS, 128)
-    bias = jnp.where(jnp.arange(TEXT) < text_len[0], 0.0, -jnp.inf).astype(F32)[None, :]
-
     vmem = pl.BlockSpec(memory_space=pltpu.VMEM)
     return pl.pallas_call(
         kernel,
         out_shape=jax.ShapeDtypeStruct(latent.shape, BF),
-        in_specs=[vmem] * 7,
+        in_specs=[vmem] * 7 + [pl.BlockSpec(memory_space=pltpu.SMEM)] + [vmem] * 2,
         out_specs=vmem,
         scratch_shapes=[
+            pltpu.VMEM((HEADS, ROWS, 256), BF),
+            pltpu.VMEM((2, ROWS, CA), BF),
+            pltpu.VMEM((2, ROWS, CB), BF),
+            pltpu.VMEM((2, TROWS, 128), BF),
             pltpu.VMEM((2, 64, D), BF),
             pltpu.VMEM((8, 2, 2, 64, D), BF),
             pltpu.VMEM((2, 64, D), BF),
@@ -563,7 +583,10 @@
             collective_id=0, has_side_effects=True, vmem_limit_bytes=60 << 20
         ),
         name="block",
-    )(latent, modulation, wsp, wa, wb, text, bias)
+    )(
+        latent, modulation, w_spatial, w_spatial_out, caption_states, w_text_kv.T, w_cross_q, text_len,
+        w_time, w_time_out,
+    )
 
 
 def solution(mesh):

time: 148 us -> 127 us (0.86)
  Pallas kernels: 137 us -> 124 us
  local copies, waits for them, and re-layouts: 8.16 us -> 1.7 us
    pallas_call x1, Pallas kernels: 137 us -> 124 us  [local(): pl.pallas_call(kernel, out_shape=jax.ShapeDtypeStruct(latent.shape, BF),...]
    unnamed x16 -> x1, local copies, waits for them, and re-layouts: 4.58 us -> 1.7 us
    reshape x10 -> x0, local copies, waits for them, and re-layouts: 2.16 us -> none  [the longest x4 1.42 us: local(): w_spatial.reshape(ROWS, 3, HEADS, HD).transpose(2, 0, 1, 3)]
where the time goes in v3:
time: 127 us
  Pallas kernels  124 us (98%)
  local copies, waits for them, and re-layouts  1.7 us (1%)
    pallas_call x1, Pallas kernels, local(): pl.pallas_call(kernel, out_shape=jax.ShapeDtypeStruct(latent.shape, BF),...  124 us

profile of v3, /device:TPU:1, one launch (start us, length us, event | category | flops | bytes accessed | tf_op | source)
XLA Modules:
  0.0 126.8 jit_solution(16251371463982921783)
XLA Ops:
  0.7 124.4 %block.1 = bf16[2,64,1152]{2,1,0:T(8,128)(2,1)} custom-call(bf16[2,64,1152]{2,1,0:T(8,128)(2,1)} %latent.1, f32[6,1152]{1,0:T(8,128)} %mod.1, bf16[36,3456]{1,0:T(8,128)(2,1)} %w_spatial.1, bf16[36,1152]{1,0:T(8,128)(2,1)} %w_out.1, bf16[300,1152]{1,0:T(8,128)(2,1)} %caption.1, bf16[72,1152]{1,0:T(8,128)(2,1)} %bitcast.1, bf16[36,1152]{1,0:T(8,128)(2,1)} %w_cross.1, ...), custom_call_target="tpu_custom_call" | custom-call | tf_op jit(solution)/shard_map/block/pallas_call | solution.py:545
  125.1 1.7 %copy.13 = bf16[2,64,1152]{2,1,0:T(8,128)(2,1)} copy(bf16[2,64,1152]{2,1,0:T(8,128)(2,1)} %block.1) | data formatting | bytes 589824

commit v4 on v3

--- a/solution.py
+++ b/solution.py
@@ -16,7 +16,8 @@
 TROWS = 40
 TEXT = 8 * TROWS
 CA = 384
-CB = 512
+CB = 384
+CW = 768
 MESH = pl.DeviceIdType.MESH
 BF = jnp.bfloat16
 F32 = jnp.float32
@@ -45,7 +46,9 @@
         return 0, tile // 2, 128 * (tile % 2)
     if tile < 24:
         return 0, tile - 16, 256
-    return 1, (tile - 24) // 4, 128 * ((tile - 24) % 4)
+    if tile < 48:
+        return 1, (tile - 24) // 3, 128 * (tile % 3)
+    return 2, 0, 128 * (tile - 48)
 
 
 def runs(first, count):
@@ -64,7 +67,7 @@
 def kernel(
     latent, mod, w_spatial, w_out, caption, w_text, w_cross, text_len, w_time, w_time_out, out,
     wsp, wa, wb, tx, nb, tok, res, s0, wqk, wvt, qb, kb, vt, scores, ot, oi,
-    za, zb, ga, gb, gt, acc, xb, qt, at, ar, rs, rr, ssem, rsem,
+    za, zb, ga, gb, gt, w2, gw, acc, xb, qt, at, ar, rs, rr, ssem, rsem,
 ):
     fr = lax.axis_index("frame")
     sp = lax.axis_index("space")
@@ -116,7 +119,7 @@
         for ref, first in ((w_out, 0), (w_cross, 9), (w_time, 18), (w_time_out, 45)):
             if t - first < ref.shape[1] // 128:
                 return ref[:, 128 * (t - first) : 128 * (t - first + 1)]
-        return jnp.zeros((ROWS, 128), BF)
+        raise ValueError(t)
 
     for quarter in range(4):
 
@@ -126,8 +129,8 @@
                 e = 2 * quarter + core
                 for i, t in enumerate((2 * e, 2 * e + 1, 16 + e)):
                     wa[core, :, 128 * i : 128 * (i + 1)] = tile_of(t)
-                for i in range(4):
-                    wb[core, :, 128 * i : 128 * (i + 1)] = tile_of(24 + 4 * e + i)
+                for i in range(3):
+                    wb[core, :, 128 * i : 128 * (i + 1)] = tile_of(24 + 3 * e + i)
             first = 2 * TROWS * quarter
             count = min(2 * TROWS, caption.shape[0] - first)
             text = nt(caption[first : first + count], w_text[...])
@@ -144,6 +147,7 @@
     for i in range(2):
         nb[i] = modulate(latent[i].astype(F32), mod[0:1], mod[1:2])
     tok[z, xl, c] = nb[xl]
+    w2[z, xl, c] = w_time_out[:, 3 * 128 :]
     res[c] = latent[c]
 
     for h in range(HEADS):
@@ -186,43 +190,50 @@
     ring_a = Ring(lambda b: za.at[b], lambda b, h: za.at[b, h])
     ring_b = Ring(lambda b: zb.at[b], lambda b, h: zb.at[b, h])
     ring_t = Ring(lambda b: gt.at[part, xl, b], lambda b, h: gt.at[part, xl, b, h])
-    ring_0 = Ring(lambda b: tok.at[b, xl, c], None)
-    ring_1 = Ring(lambda b: tok.at[b, 1 - xl, c], None)
-    tok_core = {}
-
-    def tok_ring(ring, sub, step):
-        if step < 3:
-            ring.go(step)
-        else:
-            b = block(3, 0 if sub == 0 else 1)
-            way = 0 if sub == 0 else 1
-            ref = tok.at[b, xl if sub == 0 else 1 - xl, c]
-            ring.copies[3, way] = send(ref, ref, zn[way])
-
-    def tok_share(b, lo, key):
-        ref = tok.at[b, lo, c]
-        tok_core[key] = send(ref, ref, partner)
-
-    def tok_step(step):
-        for way in range(2):
-            for sub, ring in ((0, ring_0), (1, ring_1)):
-                ring.copies[step - 1, way].wait_recv()
-        if step < 4:
-            tok_ring(ring_0, 0, step)
-            tok_ring(ring_1, 1, step)
-        for way in range(2):
+
+    class Gather:
+        def __init__(self, buf):
+            self.buf, self.shared = buf, {}
+            self.subs = (xl, 1 - xl)
+            self.rings = [Ring(lambda b, lo=lo: buf.at[b, lo, c], None) for lo in self.subs]
+
+        def go(self, sub, step):
+            if step < 3:
+                self.rings[sub].go(step)
+            else:
+                ref = self.buf.at[block(3, sub), self.subs[sub], c]
+                self.rings[sub].copies[3, sub] = send(ref, ref, zn[sub])
+
+        def share(self, step, way, sub):
+            ref = self.buf.at[block(step, way), self.subs[sub], c]
+            self.shared[step, way, sub] = send(ref, ref, partner)
+
+        def first(self, sub):
+            self.go(sub, 0)
+            self.share(0, 0, sub)
+
+        def step(self, step):
+            for way in range(2):
+                for ring in self.rings:
+                    ring.copies[step - 1, way].wait_recv()
             for sub in range(2):
-                tok_share(block(step, way), xl if sub == 0 else 1 - xl, (step, way, sub))
-
-    def tok_last():
-        ring_0.copies[3, 0].wait_recv()
-        ring_1.copies[3, 1].wait_recv()
-        tok_share(block(4, 0), xl, (4, 0, 0))
-        tok_share(block(4, 0), 1 - xl, (4, 0, 1))
-
-    def tok_ready(step, way):
-        for sub in range(2):
-            tok_core[step, way, sub].wait_recv()
+                self.go(sub, step)
+            for way in range(2):
+                for sub in range(2):
+                    self.share(step, way, sub)
+
+        def last(self):
+            for sub in range(2):
+                self.rings[sub].copies[3, sub].wait_recv()
+            for sub in range(2):
+                self.share(4, 0, sub)
+
+        def ready(self, step, way):
+            for sub in range(2):
+                self.shared[step, way, sub].wait_recv()
+
+    tokens_in = Gather(tok)
+    wide_in = Gather(w2)
 
     class Spread:
         def __init__(self, lo_rows, half_rows):
@@ -306,12 +317,10 @@
     for copy, ring in zip((init_a, init_t, init_b), rings):
         copy.wait_recv()
         ring.go(0)
-    ring_0.go(0)
-    tok_share(z, xl, (0, 0, 0))
+    tokens_in.first(0)
     weight_step(1)
     tok_x.wait_recv()
-    ring_1.go(0)
-    tok_share(z, 1 - xl, (0, 0, 1))
+    tokens_in.first(1)
     weight_step(2)
     weight_step(3)
     give_spatial(0, 1, 7, 2, 6, 3, 5, 4)
@@ -324,13 +333,14 @@
     compact(zb, gb)
     spread_b.start()
     res_in = send(latent.at[oc], res.at[c], partner)
-    tok_step(1)
+    tokens_in.step(1)
     for copy in s_in:
         copy.wait_recv()
     s_x = [
         send(s0.at[xl, pl.ds(4 * way, 4)], s0.at[xl, pl.ds(4 * way, 4)], xn[way]) for way in range(2)
     ]
-    tok_step(2)
+    wide_x = send(w2.at[z, xl, c], w2.at[z, xl, c], xmate)
+    tokens_in.step(2)
     spread_a.y_come(0)
     spread_a.y_come(1)
     spread_a.x_come(0)
@@ -343,23 +353,26 @@
     blank = jnp.zeros((D, 128 - HD), F32)
     wqk[...] = jnp.concatenate([joined[:, :HD], blank, joined[:, HD : 2 * HD], blank], axis=1).astype(BF)
     wvt[...] = jnp.concatenate([joined[:, 2 * HD : 3 * HD], blank], axis=1).T[:80].astype(BF)
-    tok_ready(0, 0)
+    tokens_in.ready(0, 0)
     qkv(z)
     for way in range(2):
-        tok_ready(1, way)
+        tokens_in.ready(1, way)
         qkv(block(1, way))
-    tok_step(3)
+    tokens_in.step(3)
     for way in range(2):
-        tok_ready(2, way)
+        tokens_in.ready(2, way)
         qkv(block(2, way))
     spread_a.y_last()
     spread_t.y_last()
     spread_b.x_come(0)
-    tok_last()
+    tokens_in.last()
+    wide_in.first(0)
+    wide_x.wait_recv()
+    wide_in.first(1)
     for way in range(2):
-        tok_ready(3, way)
+        tokens_in.ready(3, way)
         qkv(block(3, way))
-    tok_ready(4, 0)
+    tokens_in.ready(4, 0)
     qkv(block(4, 0))
     spread_a.x_come(1)
     spread_a.x_come(2)
@@ -416,9 +429,11 @@
     lax.fori_loop(2, 5, tile, 0)
     spread_a.x_come(3)
     spread_t.x_come(3)
+    wide_in.step(1)
     lax.fori_loop(5, 8, tile, 0)
     spread_b.y_last()
     spread_b.x_come(1)
+    wide_in.step(2)
     for i in range(HEADS):
         pltpu.make_async_copy(ot.at[0, 0], oi.at[i], rsem.at[oi_id + i]).wait()
 
@@ -426,7 +441,8 @@
 
     def project(rows, first, count, put):
         for at_col, buf, e, col, width in runs(first, count):
-            put(at_col, width, mm(rows, bufs[buf][e, :, col : col + width]))
+            matrix = gw[:, col : col + width] if buf == 2 else bufs[buf][e, :, col : col + width]
+            put(at_col, width, mm(rows, matrix))
 
     def put_acc(at_col, width, value):
         acc[:, at_col : at_col + width] = value
@@ -444,6 +460,7 @@
     project(after_space, 9, 9, put_qt)
     qt[:, D : D + 128] = jnp.zeros((128, 128), BF)
     spread_b.x_come(2)
+    wide_in.step(3)
     spread_t.finish()
     valid = lax.broadcasted_iota(jnp.int32, (128, TEXT), 1) < text_len[0]
     mixed = []
@@ -459,12 +476,19 @@
     after_text = (after_space.astype(F32) + crossed.astype(F32)).astype(BF)
     at[...] = after_text.reshape(16, 8, D)
 
+    wide_in.last()
     me = 2 * fr + c
     ar[me] = at[me]
     time_in = []
     for k in range(1, 16):
         p = (me + k) % 16
         time_in.append(send(at.at[p], ar.at[me], (p // 2, xl * 16 + z * 2 + p % 2)))
+    for step, way in ((0, 0), (1, 0), (1, 1), (2, 0), (2, 1), (3, 0), (3, 1), (4, 0)):
+        wide_in.ready(step, way)
+    for lo in range(2):
+        for k in range(4):
+            rows = [w2[2 * k + i // 2, lo, i % 2] for i in range(4)]
+            gw[HALF * lo + 144 * k : HALF * lo + 144 * (k + 1)] = jnp.concatenate(rows, axis=0)
     for copy in time_in:
         copy.wait_recv()
     tokens = ar[...].reshape(128, D).astype(F32)
@@ -569,6 +593,8 @@
             pltpu.VMEM((8, D, CA), BF),
             pltpu.VMEM((8, D, CB), BF),
             pltpu.VMEM((8, 2, 8, 2, TROWS, 128), BF),
+            pltpu.VMEM((8, 2, 2, ROWS, CW), BF),
+            pltpu.VMEM((D, CW), BF),
             pltpu.VMEM((128, D), F32),
             pltpu.VMEM((128, D), BF),
             pltpu.VMEM((128, 3 * D + 128), BF),

time: 127 us -> 121 us (0.953)
  Pallas kernels: 124 us -> 119 us
    pallas_call x1, Pallas kernels: 124 us -> 119 us  [local(): pl.pallas_call(kernel, out_shape=jax.ShapeDtypeStruct(latent.shape, BF),...]
where the time goes in v4:
time: 121 us
  Pallas kernels  119 us (98%)
  local copies, waits for them, and re-layouts  1.7 us (1%)
    pallas_call x1, Pallas kernels, local(): pl.pallas_call(kernel, out_shape=jax.ShapeDtypeStruct(latent.shape, BF),...  119 us

profile of v4, /device:TPU:1, one launch (start us, length us, event | category | flops | bytes accessed | tf_op | source)
XLA Modules:
  0.0 121.1 jit_solution(14023148086980713670)
XLA Ops:
  0.7 118.7 %block.1 = bf16[2,64,1152]{2,1,0:T(8,128)(2,1)} custom-call(bf16[2,64,1152]{2,1,0:T(8,128)(2,1)} %latent.1, f32[6,1152]{1,0:T(8,128)} %mod.1, bf16[36,3456]{1,0:T(8,128)(2,1)} %w_spatial.1, bf16[36,1152]{1,0:T(8,128)(2,1)} %w_out.1, bf16[300,1152]{1,0:T(8,128)(2,1)} %caption.1, bf16[72,1152]{1,0:T(8,128)(2,1)} %bitcast.1, bf16[36,1152]{1,0:T(8,128)(2,1)} %w_cross.1, ...), custom_call_target="tpu_custom_call" | custom-call | tf_op jit(solution)/shard_map/block/pallas_call | solution.py:569
  119.4 1.7 %copy.13 = bf16[2,64,1152]{2,1,0:T(8,128)(2,1)} copy(bf16[2,64,1152]{2,1,0:T(8,128)(2,1)} %block.1) | data formatting | bytes 589824

commit v5 on v4

--- a/solution.py
+++ b/solution.py
@@ -464,14 +464,15 @@
     spread_t.finish()
     valid = lax.broadcasted_iota(jnp.int32, (128, TEXT), 1) < text_len[0]
     mixed = []
+    ones = jnp.ones((TEXT, 128), BF)
     for h in range(HEADS):
         keys = gt[:, 0, h // 2, h % 2].reshape(TEXT, 128)
         values = gt[:, 1, h // 2, h % 2].reshape(TEXT, 128)
-        s = nt(qt[:, HD * h : HD * h + 128], keys) * SCALE
+        s = nt(qt[:, HD * h : HD * h + 128], keys) * (SCALE * LOG2E)
         s = jnp.where(valid, s, -jnp.inf)
-        p = jnp.exp(s - jnp.max(s, axis=-1, keepdims=True))
-        w = (p / jnp.sum(p, axis=-1, keepdims=True)).astype(BF)
-        mixed.append(mm(w, values)[:, :HD])
+        p = jnp.exp2(s - jnp.max(s, axis=-1, keepdims=True)).astype(BF)
+        both = mm(p, jnp.concatenate([values, ones], axis=1))
+        mixed.append((both[:, :128] / both[:, 128:])[:, :HD])
     crossed = jnp.concatenate(mixed, axis=1).astype(BF)
     after_text = (after_space.astype(F32) + crossed.astype(F32)).astype(BF)
     at[...] = after_text.reshape(16, 8, D)
@@ -496,21 +497,25 @@
     spread_b.x_come(3)
     spread_b.finish()
     project(xb[...], 18, 27, put_qt)
-    qt[:, 3 * D :] = jnp.zeros((128, 128), BF)
-    lanes = lax.broadcasted_iota(jnp.int32, (128, 128), 1)
-    subs = lax.broadcasted_iota(jnp.int32, (128, 128), 0)
-    same = (lanes % 8) == (subs % 8)
-    real = lanes < HD
-    mixed = []
+    lanes = lax.broadcasted_iota(jnp.int32, (128, 256), 1)
+    subs = lax.broadcasted_iota(jnp.int32, (128, 256), 0)
+    same = ((lanes % 8) == (subs % 8))[:, :128]
+    ones = jnp.ones((128, 256), BF)
+    tiles = [[] for _ in range(D // 128)]
     for h in range(HEADS):
-        q = qt[:, HD * h : HD * h + 128]
-        k = jnp.where(real, qt[:, D + HD * h : D + HD * h + 128], 0)
-        v = qt[:, 2 * D + HD * h : 2 * D + HD * h + 128]
-        s = jnp.where(same, nt(q, k) * SCALE, -jnp.inf)
-        p = jnp.exp(s - jnp.max(s, axis=-1, keepdims=True))
-        w = (p / jnp.sum(p, axis=-1, keepdims=True)).astype(BF)
-        mixed.append(mm(w, v)[:, :HD])
-    temporal = jnp.concatenate(mixed, axis=1).astype(BF)
+        first = HD * h // 128
+        width = 128 * ((HD * h + HD - 1) // 128 - first + 1)
+        base = 128 * first
+        own = jnp.logical_and(lanes >= HD * h - base, lanes < HD * (h + 1) - base)[:, :width]
+        q = qt[:, base : base + width]
+        k = jnp.where(own, qt[:, D + base : D + base + width], 0)
+        v = jnp.where(own, qt[:, 2 * D + base : 2 * D + base + width], 0)
+        s = jnp.where(same, nt(q, k) * (SCALE * LOG2E), -jnp.inf)
+        p = jnp.exp2(s - jnp.max(s, axis=-1, keepdims=True)).astype(BF)
+        o = mm(p, v) / mm(p, ones[:, :width])
+        for i in range(width // 128):
+            tiles[first + i].append(o[:, 128 * i : 128 * (i + 1)])
+    temporal = jnp.concatenate([sum(t) for t in tiles], axis=1).astype(BF)
     project(temporal, 45, 9, put_acc)
     result = (ar[...].reshape(128, D).astype(F32) + mod[5:6] * acc[...]).astype(BF)
     rs[...] = result.reshape(8, 2, 8, D)

time: 121 us -> 115 us (0.950)
  Pallas kernels: 119 us -> 113 us
    pallas_call x1, Pallas kernels: 119 us -> 113 us  [local(): pl.pallas_call(kernel, out_shape=jax.ShapeDtypeStruct(latent.shape, BF),...]
where the time goes in v5:
time: 115 us
  Pallas kernels  113 us (98%)
  local copies, waits for them, and re-layouts  1.7 us (1%)
    pallas_call x1, Pallas kernels, local(): pl.pallas_call(kernel, out_shape=jax.ShapeDtypeStruct(latent.shape, BF),...  113 us

profile of v5, /device:TPU:1, one launch (start us, length us, event | category | flops | bytes accessed | tf_op | source)
XLA Modules:
  0.0 115.1 jit_solution(17965584313695082565)
XLA Ops:
  0.7 112.7 %block.1 = bf16[2,64,1152]{2,1,0:T(8,128)(2,1)} custom-call(bf16[2,64,1152]{2,1,0:T(8,128)(2,1)} %latent.1, f32[6,1152]{1,0:T(8,128)} %mod.1, bf16[36,3456]{1,0:T(8,128)(2,1)} %w_spatial.1, bf16[36,1152]{1,0:T(8,128)(2,1)} %w_out.1, bf16[300,1152]{1,0:T(8,128)(2,1)} %caption.1, bf16[72,1152]{1,0:T(8,128)(2,1)} %bitcast.1, bf16[36,1152]{1,0:T(8,128)(2,1)} %w_cross.1, ...), custom_call_target="tpu_custom_call" | custom-call | tf_op jit(solution)/shard_map/block/pallas_call | solution.py:574
  113.4 1.7 %copy.13 = bf16[2,64,1152]{2,1,0:T(8,128)(2,1)} copy(bf16[2,64,1152]{2,1,0:T(8,128)(2,1)} %block.1) | data formatting | bytes 589824

commit v6 on v5

--- a/solution.py
+++ b/solution.py
@@ -66,7 +66,7 @@
 
 def kernel(
     latent, mod, w_spatial, w_out, caption, w_text, w_cross, text_len, w_time, w_time_out, out,
-    wsp, wa, wb, tx, nb, tok, res, s0, wqk, wvt, qb, kb, vt, scores, ot, oi,
+    wsp, wa, wb, tx, nb, tok, res, s0, wqk, wvt, qb, kb, vt, scores, odd, ot, oi,
     za, zb, ga, gb, gt, w2, gw, acc, xb, qt, at, ar, rs, rr, ssem, rsem,
 ):
     fr = lax.axis_index("frame")
@@ -395,19 +395,27 @@
             jnp.logical_and(zt == z, jnp.logical_and(xl == lo, c == xl)),
         )
 
-    def tile(i, carry):
+    fold = SCALE * LOG2E
+
+    def score(buf, k, queries, top):
+        s = nt(kb[2 * k : 2 * k + 2].reshape(512, 128), queries)
+        buf[512 * k : 512 * (k + 1)] = s
+        return jnp.maximum(top, jnp.max(s, axis=0, keepdims=True))
+
+    nothing = jnp.full((1, 256), -jnp.inf, F32)
+
+    def tile(i, now, later, top):
         zt = (z + 1 + i) % 8
-        queries = qb[zt]
-        top = jnp.full((1, 256), -jnp.inf, F32)
+        queries = qb[(z + 2 + i) % 8]
+        above = nothing
+        top = top * fold
+        total = jnp.zeros((80, 256), F32)
         for k in range(4):
-            s = nt(kb[2 * k : 2 * k + 2].reshape(512, 128), queries)
-            scores[512 * k : 512 * (k + 1)] = s
-            top = jnp.maximum(top, jnp.max(s, axis=0, keepdims=True))
-        top = top * (SCALE * LOG2E)
-        total = jnp.zeros((80, 256), F32)
-        for k in range(8):
-            p = jnp.exp2(scores[256 * k : 256 * (k + 1)] * (SCALE * LOG2E) - top)
-            total = total + mm(vt[k], p.astype(BF))
+            if later is not None:
+                above = score(later, k, queries, above)
+            for j in (2 * k, 2 * k + 1):
+                p = jnp.exp2(now[256 * j : 256 * (j + 1)] * fold - top)
+                total = total + mm(vt[j], p.astype(BF))
         mixed = (total[:HD] / total[HD : HD + 1]).astype(BF)
         for lo in range(2):
             ot[zt, lo] = mixed[:, 128 * lo : 128 * (lo + 1)]
@@ -421,16 +429,23 @@
             def _():
                 far.start()
 
-        return carry
-
-    lax.fori_loop(0, 2, tile, 0)
+        return above
+
+    def pair(i, top):
+        return tile(2 * i + 1, odd, scores, tile(2 * i, scores, odd, top))
+
+    top = nothing
+    for k in range(4):
+        top = score(scores, k, qb[(z + 1) % 8], top)
+    top = lax.fori_loop(0, 1, pair, top)
     spread_b.y_come(0)
     spread_b.y_come(1)
-    lax.fori_loop(2, 5, tile, 0)
+    top = lax.fori_loop(1, 2, pair, top)
     spread_a.x_come(3)
     spread_t.x_come(3)
     wide_in.step(1)
-    lax.fori_loop(5, 8, tile, 0)
+    top = lax.fori_loop(2, 3, pair, top)
+    tile(7, odd, None, tile(6, scores, odd, top))
     spread_b.y_last()
     spread_b.x_come(1)
     wide_in.step(2)
@@ -591,6 +606,7 @@
             pltpu.VMEM((8, 256, 128), BF),
             pltpu.VMEM((8, 80, 256), BF),
             pltpu.VMEM((2048, 256), F32),
+            pltpu.VMEM((2048, 256), F32),
             pltpu.VMEM((8, 2, HD, 128), BF),
             pltpu.VMEM((HEADS, HD, 128), BF),
             pltpu.VMEM((8, 2, ROWS, CA), BF),

time: 115 us -> 115 us (level)
  no operation moved by 1% of the time
where the time goes in v6:
time: 115 us
  Pallas kernels  112 us (97%)
  local copies, waits for them, and re-layouts  1.7 us (1%)
    pallas_call x1, Pallas kernels, local(): pl.pallas_call(kernel, out_shape=jax.ShapeDtypeStruct(latent.shape, BF),...  112 us

profile of v6, /device:TPU:1, one launch (start us, length us, event | category | flops | bytes accessed | tf_op | source)
XLA Modules:
  0.0 114.7 jit_solution(2062172854402653619)
XLA Ops:
  0.7 112.3 %block.1 = bf16[2,64,1152]{2,1,0:T(8,128)(2,1)} custom-call(bf16[2,64,1152]{2,1,0:T(8,128)(2,1)} %latent.1, f32[6,1152]{1,0:T(8,128)} %mod.1, bf16[36,3456]{1,0:T(8,128)(2,1)} %w_spatial.1, bf16[36,1152]{1,0:T(8,128)(2,1)} %w_out.1, bf16[300,1152]{1,0:T(8,128)(2,1)} %caption.1, bf16[72,1152]{1,0:T(8,128)(2,1)} %bitcast.1, bf16[36,1152]{1,0:T(8,128)(2,1)} %w_cross.1, ...), custom_call_target="tpu_custom_call" | custom-call | tf_op jit(solution)/shard_map/block/pallas_call | solution.py:589
  113.0 1.7 %copy.13 = bf16[2,64,1152]{2,1,0:T(8,128)(2,1)} copy(bf16[2,64,1152]{2,1,0:T(8,128)(2,1)} %block.1) | data formatting | bytes 589824
